TPU v7x, 256 devices: a whole 4x4x8 slice. The times are simulated.
256 devices in a mesh: row: 16 (over z, core), col: 16 (over x, y).
Axes of the slice: x: 4, y: 4, z: 8, core: 2. Of those that a mesh axis runs over, the one named last changes fastest.
Arguments:
- zblock: float32 [65536, 2048], P('row', 'col'), may hold values from -6 to 6
- reflectors: float32 [2, 65536, 256], P(None, 'row'), may hold values from -0.0234375 to 0.0234375
- tfactors: float32 [2, 256, 256], replicated, as said below
Outputs:
- eigvecs: float32 [65536, 2048], P('row', 'col')
Inputs may be any that keep to these rules, and one draw needn't show every extreme that they name: Each tfactors[b] is upper triangular with a positive diagonal.
All inputs are finite; a program needn't handle non-finite values.
Results may differ from a plain program's by a relative error of at most 0.0001.
Values sent between devices are 32-bit elements; how exact they have to be, the bound alone decides.
No kernel may reach another device: no remote copies, remote signals or barrier semaphores. Data moves between devices by JAX's collectives and lax.ppermute only.
A program may use at most 64 MiB of HBM per device.

v0:
```python
import jax
import jax.numpy as jnp
from jax import lax
from jax.sharding import PartitionSpec as P


def hdot(left, right):
    return jnp.dot(left, right, precision=lax.Precision.HIGHEST, preferred_element_type=jnp.float32)


def body(zblock, reflectors, tfactors):
    current = zblock
    for index in (1, 0):
        vblock = reflectors[index]
        partial_value = hdot(vblock.T, current)
        summed = lax.psum(partial_value, "row")
        current = current - hdot(vblock, hdot(tfactors[index], summed))
    return current


def solution(mesh):
    in_specs = (P("row", "col"), P(None, "row", None), P())
    out_specs = P("row", "col")
    return jax.shard_map(body, mesh=mesh, in_specs=in_specs, out_specs=out_specs, check_vma=False)
```

profile of v0, /device:TPU:1, one launch (start us, length us, event | category | flops | bytes accessed | tf_op | source)
XLA Modules:
  0.0 266.5 jit_solution(8444827076382217478)
XLA Ops:
  6.5 0.0 copy-start.1
  6.5 0.0 copy-start.2
  6.5 0.0 all-reduce.3.cloned.1.call-start
  6.5 10.3 %fusion.6 = f32[256,128]{1,0:T(8,128)} fusion(f32[4096,128]{1,0:T(8,128)} %param.3, f32[2,4096,256]{2,1,0:T(8,128)} %param.4), kind=kOutput, calls=%fused_computation.8 | convolution fusion | flops 1610612736 | bytes 6422528 | tf_op jit(solution)/shard_map/dot_general | solution.py:8
  16.8 0.0 all-reduce.3.cloned.1.call-update
  16.9 0.2 all-reduce.5.cloned.1.call-start
  17.1 0.0 copy-done.1
  17.1 1.8 copy.4
  18.9 109.4 %all-reduce.3.cloned.1.call-done = f32[256,128]{1,0:T(8,128)} async-done(((f32[256,128]{1,0:T(8,128)}), f32[256,128]{1,0:T(8,128)}) %all-reduce.3.cloned.1.call-update) | async-done | bytes 131088 | tf_op jit(solution)/shard_map/psum | solution.py:16
  128.3 0.0 copy-done.2
  128.3 1.3 fusion.17
  129.6 0.0 copy-start
  129.6 7.3 %fusion.1 = f32[4096,128]{0,1:T(8,128)S(1)} fusion(f32[4096,128]{0,1:T(8,128)} %copy.4, f32[128,256]{1,0:T(8,128)S(1)} %fusion.17, f32[2,4096,256]{2,1,0:T(8,128)} %param.4), kind=kOutput, calls=%fused_computation.3 | convolution fusion | flops 1611137024 | bytes 8519680 | tf_op jit(solution)/shard_map/dot_general | solution.py:8
  136.9 0.0 copy-done
  136.9 2.8 %fusion.12 = f32[256,128]{0,1:T(8,128)} fusion(f32[4096,128]{0,1:T(8,128)S(1)} %fusion.1, f32[2,4096,256]{2,1,0:T(8,128)S(1)} %copy-done), kind=kOutput, calls=%fused_computation.14 | convolution fusion | flops 1610612736 | bytes 6422528 | tf_op jit(solution)/shard_map/dot_general | solution.py:8
  139.7 0.0 all-reduce.5.cloned.1.call-update
  139.7 107.9 %all-reduce.5.cloned.1.call-done = f32[256,128]{0,1:T(8,128)} async-done(((f32[256,128]{0,1:T(8,128)}), f32[256,128]{0,1:T(8,128)}) %all-reduce.5.cloned.1.call-update) | async-done | bytes 131088 | tf_op jit(solution)/shard_map/psum | solution.py:16
  247.7 1.3 fusion.15
  249.0 7.8 %fusion = f32[4096,128]{0,1:T(8,128)} fusion(f32[4096,128]{0,1:T(8,128)S(1)} %fusion.1, f32[128,256]{1,0:T(8,128)S(1)} %fusion.15, f32[2,4096,256]{2,1,0:T(8,128)} %param.4), kind=kOutput, calls=%fused_computation.1 | convolution fusion | flops 1611137024 | bytes 8519680 | tf_op jit(solution)/shard_map/dot_general | solution.py:8
  256.8 2.9 %copy.5 = f32[4096,128]{1,0:T(8,128)} copy(f32[4096,128]{0,1:T(8,128)} %fusion) | data formatting | bytes 4194304 | tf_op jit(solution)/shard_map/sub | solution.py:17
Async XLA Ops:
  6.5 10.6 %copy-start.1 = (f32[4096,128]{1,0:T(8,128)S(1)}, f32[4096,128]{1,0:T(8,128)}, u32[]{:S(2)}) copy-start(f32[4096,128]{1,0:T(8,128)} %param.3) | copy-start | bytes 6291460
  6.5 121.7 %copy-start.2 = (f32[2,256,256]{2,1,0:T(8,128)S(1)}, f32[2,256,256]{2,1,0:T(8,128)}, u32[]{:S(2)}) copy-start(f32[2,256,256]{2,1,0:T(8,128)} %param.5) | copy-start | bytes 1572868
  6.5 121.7 %all-reduce.3.cloned.1.call-start = ((), (), s32[]{:S(2)}) async-start(), calls=%async_computation | async-start | bytes 262144 | tf_op jit(solution)/shard_map/psum | solution.py:16
  16.9 230.8 %all-reduce.5.cloned.1.call-start = ((), (), s32[]{:S(2)}) async-start(), calls=%async_computation.1 | async-start | bytes 262144 | tf_op jit(solution)/shard_map/psum | solution.py:16
  129.6 7.3 %copy-start = (f32[2,4096,256]{2,1,0:T(8,128)S(1)}, f32[2,4096,256]{2,1,0:T(8,128)}, u32[]{:S(2)}) copy-start(f32[2,4096,256]{2,1,0:T(8,128)} %param.4) | copy-start | bytes 25165828
Sparse Core Ops, SparseCore 0:
  17.0 111.2 all-reduce.2
  139.8 107.7 all-reduce.4
where the time goes:
time: 267 us; the launch traced here: 266 us
  waiting for transfers between devices  217 us (81%)
  matrix products  30.8 us (12%)
  between operations  13.5 us (5%)
  local copies, waits for them, and re-layouts  4.7 us (2%)
    psum x2, waiting for transfers between devices, body(): summed = lax.psum(partial_value, 'row')  217 us
    dot_general x6, matrix products, hdot(): jnp.dot(left, right, precision=lax.Precision.HIGHEST, preferred_element_t...  30.8 us
  transfers between devices with their start and end apart: 2, of which 2 were waited for; matrix products, arithmetic and copies ran while one was open for 1% of the time, Pallas kernels for 0%

commit v1 on v0

v1 whole, which is shorter than its diff:
```python
import jax
import jax.numpy as jnp
from jax import lax
from jax.sharding import PartitionSpec as P

HIGH = lax.Precision.HIGH


def dot(left, right, dims):
    return lax.dot_general(left, right, ((dims[:1], dims[1:]), ((), ())), precision=HIGH, preferred_element_type=jnp.float32)


def pairs_of(first, second, chips):
    return [(2 * z + core, 2 * (step(z) % chips) + core) for z in range(chips) for core, step in ((0, first), (1, second))]


def aligned(z):
    return z ^ 1


def shifted(z):
    return ((z + 1) ^ 1) - 1


def across(z):
    return z + 3 if z % 2 == 0 else z - 3


def across_back(z):
    return z - 3 if z % 2 == 0 else z + 3


def halves_summed(value, core, swap):
    half = value.shape[0] // 2
    own = lax.dynamic_slice_in_dim(value, core * half, half, 0)
    other = lax.dynamic_slice_in_dim(value, (1 - core) * half, half, 0)
    return own + lax.ppermute(other, "row", swap)


def joined(value, core, swap):
    other = lax.ppermute(value, "row", swap)
    return jnp.where(core == 0, jnp.concatenate([value, other], 0), jnp.concatenate([other, value], 0))


def sums_over_row(values, chips):
    core = lax.axis_index("row") % 2
    swap = [(i, i ^ 1) for i in range(2 * chips)]
    steps = [pairs_of(aligned, shifted, chips), pairs_of(shifted, aligned, chips), pairs_of(across, across_back, chips)]
    parts = [halves_summed(value, core, swap) for value in values]
    for step in steps:
        parts = [part + lax.ppermute(part, "row", step) for part in parts]
    return [joined(part, core, swap) for part in parts]


def body(zblock, reflectors, tfactors):
    v0, v1 = reflectors[0], reflectors[1]
    gram = dot(v0, v1, (0, 0))
    first = dot(v1, zblock, (0, 0))
    second = dot(v0, zblock, (0, 0))
    gram = jnp.concatenate([gram[:, :128], gram[:, 128:]], 0)
    gram, products = sums_over_row([gram, jnp.concatenate([first, second], 0)], 8)
    gram = jnp.concatenate([gram[:256], gram[256:]], 1)
    lead = dot(tfactors[1], products[:256], (1, 0))
    tail = dot(tfactors[0], products[256:] - dot(gram, lead, (1, 0)), (1, 0))
    return zblock - dot(v1, lead, (1, 0)) - dot(v0, tail, (1, 0))


def solution(mesh):
    in_specs = (P("row", "col"), P(None, "row", None), P())
    out_specs = P("row", "col")
    return jax.shard_map(body, mesh=mesh, in_specs=in_specs, out_specs=out_specs, check_vma=False)
```

time: 267 us -> 61.3 us (0.23)
  waiting for transfers between devices: 217 us -> 8.77 us
  starting transfers between devices: 0.22 us -> 20 us
  between operations: 13.5 us -> 0.19 us
  matrix products: 30.8 us -> 27.9 us
    psum x2 -> x0, waiting for transfers between devices: 217 us -> none  [body(): summed = lax.psum(partial_value, 'row')]
    ppermute x0 -> x10, starting transfers between devices: none -> 20 us  [the longest x6 10.2 us: sums_over_row(): parts = [part + lax.ppermute(part, 'row', step) for part in parts]]
    ppermute x0 -> x10, waiting for transfers between devices: none -> 8.77 us  [the longest x6 7.83 us: sums_over_row(): parts = [part + lax.ppermute(part, 'row', step) for part in parts]]
    dot_general x6 -> x8, matrix products: 30.8 us -> 27.9 us  [dot(): lax.dot_general(left, right, ((dims[:1], dims[1:]), ((), ())), precision=...]
  transfers between devices with their start and end apart: 2 -> 10, of which waited for: 2 -> 7; matrix products, arithmetic and copies ran while one was open for 1% -> 22% of each run, Pallas kernels for 0% -> 0%
where the time goes in v1:
time: 61.3 us; the launch traced here: 61 us
  matrix products  27.9 us (46%)
  starting transfers between devices  20 us (33%)
  waiting for transfers between devices  8.77 us (14%)
  local copies, waits for them, and re-layouts  3.67 us (6%)
    dot_general x8, matrix products, dot(): lax.dot_general(left, right, ((dims[:1], dims[1:]), ((), ())), precision=...  27.9 us
    ppermute x6, starting transfers between devices, sums_over_row(): parts = [part + lax.ppermute(part, 'row', step) for part in parts]  10.2 us
    ppermute x6, waiting for transfers between devices, sums_over_row(): parts = [part + lax.ppermute(part, 'row', step) for part in parts]  7.83 us
    ppermute x2, starting transfers between devices, joined(): other = lax.ppermute(value, 'row', swap)  6.38 us
    ppermute x2, starting transfers between devices, halves_summed(): return own + lax.ppermute(other, 'row', swap)  3.44 us
    unnamed x7, local copies, waits for them, and re-layouts  1.82 us
    sub x1, local copies, waits for them, and re-layouts, body(): return zblock - dot(v1, lead, (1, 0)) - dot(v0, tail, (1, 0))  1.81 us
  transfers between devices with their start and end apart: 10, of which 7 were waited for; matrix products, arithmetic and copies ran while one was open for 22% of the time, Pallas kernels for 0%

profile of v1, /device:TPU:1, one launch (start us, length us, event | category | flops | bytes accessed | tf_op | source)
XLA Modules:
  0.0 61.0 jit_solution(16110437295338621609)
XLA Ops:
  0.0 0.0 copy-start
  0.0 7.0 %fusion.3 = f32[256,256]{1,0:T(8,128)S(1)} fusion(f32[2,4096,256]{2,1,0:T(8,128)} %param.4), kind=kOutput, calls=%fused_computation.5 | convolution fusion | flops 1610612736 | bytes 8650752 | tf_op jit(solution)/shard_map/dot_general | solution.py:10
  7.1 0.1 fusion.27
  7.2 3.3 %collective-permute-start.5 = (f32[256,128]{1,0:T(8,128)S(1)}, f32[256,128]{1,0:T(8,128)S(1)}, u32[]{:S(2)}, u32[]{:S(2)}) collective-permute-start(f32[256,128]{1,0:T(8,128)S(1)} %fusion.27), channel_id=1, source_target_pairs={{0,16},{16,0},{32,48},{48,32},{64,80},{80,64},{96,112},{112,96},{1... | collective-permute-start | bytes 393224 | tf_op jit(solution)/shard_map/ppermute | solution.py:37
  10.5 0.0 copy-done
  10.5 5.6 %fusion.9 = f32[256,128]{1,0:T(8,128)S(1)} fusion(f32[4096,128]{1,0:T(8,128)S(1)} %copy-done, f32[2,4096,256]{2,1,0:T(8,128)} %param.4), kind=kOutput, calls=%fused_computation.11 | convolution fusion | flops 805306368 | bytes 6422528 | tf_op jit(solution)/shard_map/dot_general | solution.py:10
  16.1 5.6 %fusion.5 = f32[256,128]{1,0:T(8,128)S(1)} fusion(f32[4096,128]{1,0:T(8,128)S(1)} %copy-done, f32[2,4096,256]{2,1,0:T(8,128)} %param.4), kind=kOutput, calls=%fused_computation.7 | convolution fusion | flops 805306368 | bytes 6422528 | tf_op jit(solution)/shard_map/dot_general | solution.py:10
  21.7 0.1 fusion.30
  21.8 0.1 collective-permute-start
  21.9 0.0 collective-permute-done.5
  21.9 0.1 fusion.29
  22.0 3.9 %collective-permute-start.6 = (f32[256,128]{1,0:T(8,128)S(1)}, f32[256,128]{1,0:T(8,128)S(1)}, u32[]{:S(2)}, u32[]{:S(2)}) collective-permute-start(f32[256,128]{1,0:T(8,128)S(1)} %fusion.29), channel_id=1, source_target_pairs={{0,32},{16,240},{32,0},{48,80},{64,96},{80,48},{96,64},{112,144},{... | collective-permute-start | bytes 393224 | tf_op jit(solution)/shard_map/ppermute | solution.py:51
  25.9 0.0 collective-permute-done
  25.9 0.1 fusion.32
  26.0 0.0 copy-start.2
  26.0 1.4 %collective-permute-start.1 = (f32[256,128]{1,0:T(8,128)S(1)}, f32[256,128]{1,0:T(8,128)S(1)}, u32[]{:S(2)}, u32[]{:S(2)}) collective-permute-start(f32[256,128]{1,0:T(8,128)S(1)} %fusion.32), channel_id=1, source_target_pairs={{0,32},{16,240},{32,0},{48,80},{64,96},{80,48},{96,64},{112,144},{... | collective-permute-start | bytes 393224 | tf_op jit(solution)/shard_map/ppermute | solution.py:51
  27.4 0.9 %collective-permute-done.6 = f32[256,128]{1,0:T(8,128)S(1)} collective-permute-done((f32[256,128]{1,0:T(8,128)S(1)}, f32[256,128]{1,0:T(8,128)S(1)}, u32[]{:S(2)}, u32[]{:S(2)}) %collective-permute-start.6) | collective-permute-done | bytes 131104 | tf_op jit(solution)/shard_map/ppermute | solution.py:51
  28.3 0.1 collective-permute-start.7
  28.4 2.9 %collective-permute-done.1 = f32[256,128]{1,0:T(8,128)S(1)} collective-permute-done((f32[256,128]{1,0:T(8,128)S(1)}, f32[256,128]{1,0:T(8,128)S(1)}, u32[]{:S(2)}, u32[]{:S(2)}) %collective-permute-start.1) | collective-permute-done | bytes 131104 | tf_op jit(solution)/shard_map/ppermute | solution.py:51
  31.4 0.1 collective-permute-start.2
  31.5 0.8 %collective-permute-done.7 = f32[256,128]{1,0:T(8,128)S(1)} collective-permute-done((f32[256,128]{1,0:T(8,128)S(1)}, f32[256,128]{1,0:T(8,128)S(1)}, u32[]{:S(2)}, u32[]{:S(2)}) %collective-permute-start.7) | collective-permute-done | bytes 131104 | tf_op jit(solution)/shard_map/ppermute | solution.py:51
  32.2 2.9 %collective-permute-start.8 = (f32[256,128]{1,0:T(8,128)S(1)}, f32[256,128]{1,0:T(8,128)S(1)}, u32[]{:S(2)}, u32[]{:S(2)}) collective-permute-start(f32[256,128]{1,0:T(8,128)S(1)} %add.45), channel_id=1, source_target_pairs={{0,96},{16,176},{32,192},{48,144},{64,160},{80,240},{96,0},{112,20... | collective-permute-start | bytes 393224 | tf_op jit(solution)/shard_map/ppermute | solution.py:51
  35.2 0.1 collective-permute-done.2
  35.3 1.7 %collective-permute-start.3 = (f32[256,128]{1,0:T(8,128)S(1)}, f32[256,128]{1,0:T(8,128)S(1)}, u32[]{:S(2)}, u32[]{:S(2)}) collective-permute-start(f32[256,128]{1,0:T(8,128)S(1)} %add.41), channel_id=1, source_target_pairs={{0,96},{16,176},{32,192},{48,144},{64,160},{80,240},{96,0},{112,20... | collective-permute-start | bytes 393224 | tf_op jit(solution)/shard_map/ppermute | solution.py:51
  37.0 2.3 %collective-permute-done.8 = f32[256,128]{1,0:T(8,128)S(1)} collective-permute-done((f32[256,128]{1,0:T(8,128)S(1)}, f32[256,128]{1,0:T(8,128)S(1)}, u32[]{:S(2)}, u32[]{:S(2)}) %collective-permute-start.8) | collective-permute-done | bytes 131104 | tf_op jit(solution)/shard_map/ppermute | solution.py:51
  39.4 4.5 %collective-permute-start.9 = (f32[256,128]{1,0:T(8,128)S(1)}, f32[256,128]{1,0:T(8,128)S(1)}, u32[]{:S(2)}, u32[]{:S(2)}) collective-permute-start(f32[256,128]{1,0:T(8,128)S(1)} %add.46), channel_id=1, source_target_pairs={{0,16},{16,0},{32,48},{48,32},{64,80},{80,64},{96,112},{112,96},{1... | collective-permute-start | bytes 393224 | tf_op jit(solution)/shard_map/ppermute | solution.py:41
  43.9 1.8 %copy.4 = f32[4096,128]{0,1:T(8,128)} copy(f32[4096,128]{1,0:T(8,128)S(1)} %copy-done) | data formatting | bytes 4194304 | tf_op args[0]
  45.7 0.0 copy-start.1
  45.7 0.9 %collective-permute-done.3 = f32[256,128]{1,0:T(8,128)S(1)} collective-permute-done((f32[256,128]{1,0:T(8,128)S(1)}, f32[256,128]{1,0:T(8,128)S(1)}, u32[]{:S(2)}, u32[]{:S(2)}) %collective-permute-start.3) | collective-permute-done | bytes 131104 | tf_op jit(solution)/shard_map/ppermute | solution.py:51
  46.5 1.9 %collective-permute-start.4 = (f32[256,128]{1,0:T(8,128)S(1)}, f32[256,128]{1,0:T(8,128)S(1)}, u32[]{:S(2)}, u32[]{:S(2)}) collective-permute-start(f32[256,128]{1,0:T(8,128)S(1)} %add.42), channel_id=1, source_target_pairs={{0,16},{16,0},{32,48},{48,32},{64,80},{80,64},{96,112},{112,96},{1... | collective-permute-start | bytes 393224 | tf_op jit(solution)/shard_map/ppermute | solution.py:41
  48.4 0.0 collective-permute-done.9
  48.5 0.9 %collective-permute-done.4 = f32[256,128]{1,0:T(8,128)S(1)} collective-permute-done((f32[256,128]{1,0:T(8,128)S(1)}, f32[256,128]{1,0:T(8,128)S(1)}, u32[]{:S(2)}, u32[]{:S(2)}) %collective-permute-start.4) | collective-permute-done | bytes 131104 | tf_op jit(solution)/shard_map/ppermute | solution.py:41
  49.4 0.0 copy-done.2
  49.5 0.3 fusion.23
  49.8 0.3 fusion.17
  50.0 0.3 fusion.21
  50.4 0.0 copy-done.1
  50.4 4.4 %fusion.1 = f32[4096,128]{0,1:T(8,128)S(1)} fusion(f32[4096,128]{0,1:T(8,128)S(1)} %copy-done.1, f32[128,256]{1,0:T(8,128)S(1)} %fusion.23, f32[2,4096,256]{2,1,0:T(8,128)} %param.4), kind=kOutput, calls=%fused_computation.3 | convolution fusion | flops 805830656 | bytes 8519680 | tf_op jit(solution)/shard_map/dot_general | solution.py:10
  54.8 4.4 %fusion = f32[4096,128]{0,1:T(8,128)S(1)} fusion(f32[4096,128]{0,1:T(8,128)S(1)} %fusion.1, f32[128,256]{1,0:T(8,128)S(1)} %fusion.21, f32[2,4096,256]{2,1,0:T(8,128)} %param.4), kind=kOutput, calls=%fused_computation.1 | convolution fusion | flops 805830656 | bytes 8519680 | tf_op jit(solution)/shard_map/dot_general | solution.py:10
  59.2 1.8 %copy.5 = f32[4096,128]{1,0:T(8,128)} copy(f32[4096,128]{0,1:T(8,128)S(1)} %fusion) | data formatting | bytes 4194304 | tf_op jit(solution)/shard_map/sub | solution.py:65
  (10 shorter events, 0.2 us)
Async XLA Ops:
  0.0 10.5 %copy-start = (f32[4096,128]{1,0:T(8,128)S(1)}, f32[4096,128]{1,0:T(8,128)}, u32[]{:S(2)}) copy-start(f32[4096,128]{1,0:T(8,128)} %param.3) | copy-start | bytes 6291460
  7.2 14.8 %collective-permute-start.5 = (f32[256,128]{1,0:T(8,128)S(1)}, f32[256,128]{1,0:T(8,128)S(1)}, u32[]{:S(2)}, u32[]{:S(2)}) collective-permute-start(f32[256,128]{1,0:T(8,128)S(1)} %fusion.27), channel_id=1, source_target_pairs={{0,16},{16,0},{32,48},{48,32},{64,80},{80,64},{96,112},{112,96},{1... | collective-permute-start | bytes 393224 | tf_op jit(solution)/shard_map/ppermute | solution.py:37
  21.8 4.1 %collective-permute-start = (f32[256,128]{1,0:T(8,128)S(1)}, f32[256,128]{1,0:T(8,128)S(1)}, u32[]{:S(2)}, u32[]{:S(2)}) collective-permute-start(f32[256,128]{1,0:T(8,128)S(1)} %fusion.30), channel_id=1, source_target_pairs={{0,16},{16,0},{32,48},{48,32},{64,80},{80,64},{96,112},{112,96},{1... | collective-permute-start | bytes 393224 | tf_op jit(solution)/shard_map/ppermute | solution.py:37
  22.0 6.3 %collective-permute-start.6 = (f32[256,128]{1,0:T(8,128)S(1)}, f32[256,128]{1,0:T(8,128)S(1)}, u32[]{:S(2)}, u32[]{:S(2)}) collective-permute-start(f32[256,128]{1,0:T(8,128)S(1)} %fusion.29), channel_id=1, source_target_pairs={{0,32},{16,240},{32,0},{48,80},{64,96},{80,48},{96,64},{112,144},{... | collective-permute-start | bytes 393224 | tf_op jit(solution)/shard_map/ppermute | solution.py:51
  26.0 23.4 %copy-start.2 = (f32[2,256,256]{2,1,0:T(8,128)S(1)}, f32[2,256,256]{2,1,0:T(8,128)}, u32[]{:S(2)}) copy-start(f32[2,256,256]{2,1,0:T(8,128)} %param.5) | copy-start | bytes 1572868
  26.0 5.3 %collective-permute-start.1 = (f32[256,128]{1,0:T(8,128)S(1)}, f32[256,128]{1,0:T(8,128)S(1)}, u32[]{:S(2)}, u32[]{:S(2)}) collective-permute-start(f32[256,128]{1,0:T(8,128)S(1)} %fusion.32), channel_id=1, source_target_pairs={{0,32},{16,240},{32,0},{48,80},{64,96},{80,48},{96,64},{112,144},{... | collective-permute-start | bytes 393224 | tf_op jit(solution)/shard_map/ppermute | solution.py:51
  28.3 3.9 %collective-permute-start.7 = (f32[256,128]{1,0:T(8,128)S(1)}, f32[256,128]{1,0:T(8,128)S(1)}, u32[]{:S(2)}, u32[]{:S(2)}) collective-permute-start(f32[256,128]{1,0:T(8,128)S(1)} %add.44), channel_id=1, source_target_pairs={{0,224},{16,48},{32,64},{48,16},{64,32},{80,112},{96,128},{112,80}... | collective-permute-start | bytes 393224 | tf_op jit(solution)/shard_map/ppermute | solution.py:51
  31.4 3.9 %collective-permute-start.2 = (f32[256,128]{1,0:T(8,128)S(1)}, f32[256,128]{1,0:T(8,128)S(1)}, u32[]{:S(2)}, u32[]{:S(2)}) collective-permute-start(f32[256,128]{1,0:T(8,128)S(1)} %add.40), channel_id=1, source_target_pairs={{0,224},{16,48},{32,64},{48,16},{64,32},{80,112},{96,128},{112,80}... | collective-permute-start | bytes 393224 | tf_op jit(solution)/shard_map/ppermute | solution.py:51
  32.2 7.1 %collective-permute-start.8 = (f32[256,128]{1,0:T(8,128)S(1)}, f32[256,128]{1,0:T(8,128)S(1)}, u32[]{:S(2)}, u32[]{:S(2)}) collective-permute-start(f32[256,128]{1,0:T(8,128)S(1)} %add.45), channel_id=1, source_target_pairs={{0,96},{16,176},{32,192},{48,144},{64,160},{80,240},{96,0},{112,20... | collective-permute-start | bytes 393224 | tf_op jit(solution)/shard_map/ppermute | solution.py:51
  35.3 11.2 %collective-permute-start.3 = (f32[256,128]{1,0:T(8,128)S(1)}, f32[256,128]{1,0:T(8,128)S(1)}, u32[]{:S(2)}, u32[]{:S(2)}) collective-permute-start(f32[256,128]{1,0:T(8,128)S(1)} %add.41), channel_id=1, source_target_pairs={{0,96},{16,176},{32,192},{48,144},{64,160},{80,240},{96,0},{112,20... | collective-permute-start | bytes 393224 | tf_op jit(solution)/shard_map/ppermute | solution.py:51
  39.4 9.1 %collective-permute-start.9 = (f32[256,128]{1,0:T(8,128)S(1)}, f32[256,128]{1,0:T(8,128)S(1)}, u32[]{:S(2)}, u32[]{:S(2)}) collective-permute-start(f32[256,128]{1,0:T(8,128)S(1)} %add.46), channel_id=1, source_target_pairs={{0,16},{16,0},{32,48},{48,32},{64,80},{80,64},{96,112},{112,96},{1... | collective-permute-start | bytes 393224 | tf_op jit(solution)/shard_map/ppermute | solution.py:41
  45.7 4.7 %copy-start.1 = (f32[4096,128]{0,1:T(8,128)S(1)}, f32[4096,128]{0,1:T(8,128)}, u32[]{:S(2)}) copy-start(f32[4096,128]{0,1:T(8,128)} %copy.4) | copy-start | bytes 6291460
  46.5 2.9 %collective-permute-start.4 = (f32[256,128]{1,0:T(8,128)S(1)}, f32[256,128]{1,0:T(8,128)S(1)}, u32[]{:S(2)}, u32[]{:S(2)}) collective-permute-start(f32[256,128]{1,0:T(8,128)S(1)} %add.42), channel_id=1, source_target_pairs={{0,16},{16,0},{32,48},{48,32},{64,80},{80,64},{96,112},{112,96},{1... | collective-permute-start | bytes 393224 | tf_op jit(solution)/shard_map/ppermute | solution.py:41

commit v2 on v0

v2 whole, which is shorter than its diff:
```python
import functools

import jax
import jax.numpy as jnp
from jax import lax
from jax.experimental import pallas as pl
from jax.experimental.pallas import tpu as pltpu
from jax.sharding import PartitionSpec as P

F32 = jnp.float32
BF16 = jnp.bfloat16
HBM = pl.BlockSpec(memory_space=pl.ANY)
VMEM = pl.BlockSpec(memory_space=pltpu.VMEM)
CHUNKS = 8
MIB = 2**20


def split(value):
    high = value.astype(BF16)
    return high, (value - high.astype(F32)).astype(BF16)


def mm(left, right):
    return jnp.dot(left, right, preferred_element_type=F32)


def exact(left, right, right_dim):
    dims = (((1,), (right_dim,)), ((), ()))
    return lax.dot_general(left, right, dims, precision=lax.Precision.HIGHEST, preferred_element_type=F32)


def call(kernel, ins, outs, scratch, limit, flops):
    cost = pl.CostEstimate(flops=flops, bytes_accessed=4 * MIB, transcendentals=0)
    params = pltpu.CompilerParams(vmem_limit_bytes=limit * MIB)
    specs = [HBM if getattr(shape, "memory_space", None) is None else VMEM for shape in outs]
    return pl.pallas_call(kernel, in_specs=ins, out_specs=specs, out_shape=outs, scratch_shapes=scratch, compiler_params=params, cost_estimate=cost)


def products_kernel(z_hbm, v_hbm, first_ref, second_ref, high_ref, low_ref, z_ref, v_ref, sems):
    rows = z_ref.shape[0] // CHUNKS
    copies = []
    for k in range(CHUNKS):
        part = pl.ds(k * rows, rows)
        group = [pltpu.make_async_copy(z_hbm.at[part], z_ref.at[part], sems.at[k, 2])]
        group += [pltpu.make_async_copy(v_hbm.at[b, part], v_ref.at[b, part], sems.at[k, b]) for b in (1, 0)]
        for copy in group:
            copy.start()
        copies.append(group)
    totals = [None, None]
    for k in range(CHUNKS):
        part = pl.ds(k * rows, rows)
        for copy in copies[k]:
            copy.wait()
        z_high, z_low = split(z_ref[part, :].T)
        z_both = jnp.concatenate([z_high, z_low], 0)
        for b in (1, 0):
            high, low = split(v_ref[b, part, :])
            high_ref[b, part, :] = high
            low_ref[b, part, :] = low
            both = mm(z_both, high)
            term = both[:128] + both[128:] + mm(z_high, low)
            totals[b] = term if k == 0 else totals[b] + term
    first_ref[...] = totals[1]
    second_ref[...] = totals[0]


def gram_kernel(high_ref, low_ref, upper_ref, lower_ref):
    rows = high_ref.shape[1] // CHUNKS
    total = None
    for k in range(CHUNKS):
        part = pl.ds(k * rows, rows)
        left = jnp.concatenate([high_ref[1, part, :].T, low_ref[1, part, :].T], 0)
        both = mm(left, high_ref[0, part, :])
        term = both[:256] + both[256:] + mm(left[:256], low_ref[0, part, :])
        total = term if k == 0 else total + term
    upper_ref[...] = total[:128]
    lower_ref[...] = total[128:]


def widened(value):
    return jnp.concatenate(split(value.T), 1)


def updated(base, high, low, wide):
    both = mm(high, wide) + mm(low, wide)
    return base - (both[:, :128] + both[:, 128:])


def lead_kernel(z_ref, high_ref, low_ref, t_ref, first_ref, lead_ref, base_ref):
    lead = exact(first_ref[...], t_ref[1], 1)
    lead_ref[...] = lead
    wide = widened(lead)
    rows = z_ref.shape[0] // CHUNKS
    for k in range(CHUNKS):
        part = pl.ds(k * rows, rows)
        base_ref[part, :] = updated(z_ref[part, :], high_ref[1, part, :], low_ref[1, part, :], wide)


def tail_kernel(base_ref, high_ref, low_ref, t_ref, lead_ref, second_ref, gram_ref, out_hbm, out_ref, sems):
    tail = exact(second_ref[...] - exact(lead_ref[...], gram_ref[...], 0), t_ref[0], 1)
    wide = widened(tail)
    rows = base_ref.shape[0] // CHUNKS
    copies = []
    for k in range(CHUNKS):
        part = pl.ds(k * rows, rows)
        out_ref[part, :] = updated(base_ref[part, :], high_ref[0, part, :], low_ref[0, part, :], wide)
        copy = pltpu.make_async_copy(out_ref.at[part], out_hbm.at[part], sems.at[k])
        copy.start()
        copies.append(copy)
    for copy in copies:
        copy.wait()


def pairs_of(first, second, chips):
    return [(2 * z + core, 2 * (step(z) % chips) + core) for z in range(chips) for core, step in ((0, first), (1, second))]


def aligned(z):
    return z ^ 1


def shifted(z):
    return ((z + 1) ^ 1) - 1


def across(z):
    return z + 3 if z % 2 == 0 else z - 3


def across_back(z):
    return z - 3 if z % 2 == 0 else z + 3


def sums_over_row(pairs, chips):
    even = lax.axis_index("row") % 2 == 0
    swap = [(i, i ^ 1) for i in range(2 * chips)]
    steps = [pairs_of(aligned, shifted, chips), pairs_of(shifted, aligned, chips), pairs_of(across, across_back, chips)]
    parts = [jnp.where(even, one, two) + lax.ppermute(jnp.where(even, two, one), "row", swap) for one, two in pairs]
    for step in steps:
        parts = [part + lax.ppermute(part, "row", step) for part in parts]
    results = []
    for part in parts:
        other = lax.ppermute(part, "row", swap)
        results.append((jnp.where(even, part, other), jnp.where(even, other, part)))
    return results


def body(zblock, reflectors, tfactors):
    rows, columns = zblock.shape
    width = reflectors.shape[2]
    product = pltpu.VMEM((columns, width), F32)
    halves = pltpu.VMEM(reflectors.shape, BF16)
    whole = pltpu.VMEM(zblock.shape, F32)
    work = 6 * rows * columns * width
    first, second, high, low, zblock = call(
        products_kernel,
        [HBM, HBM],
        [product, product, halves, halves, whole],
        [pltpu.VMEM(reflectors.shape, F32), pltpu.SemaphoreType.DMA((CHUNKS, 3))],
        44,
        2 * work,
    )(zblock, reflectors)
    upper, lower = call(gram_kernel, [VMEM] * 2, [product, product], [], 16, 2 * work)(high, low)
    (first, second), (upper, lower) = sums_over_row([(first, second), (upper, lower)], 8)
    lead, base = call(lead_kernel, [VMEM] * 5, [product, whole], [], 16, work)(zblock, high, low, tfactors, first)
    gram = jnp.concatenate([upper, lower], 0)
    result = jax.ShapeDtypeStruct(zblock.shape, F32)
    scratch = [whole, pltpu.SemaphoreType.DMA((CHUNKS,))]
    return call(tail_kernel, [VMEM] * 7, [result], scratch, 16, work)(base, high, low, tfactors, lead, second, gram)[0]


def solution(mesh):
    in_specs = (P("row", "col"), P(None, "row", None), P())
    out_specs = P("row", "col")
    return jax.shard_map(body, mesh=mesh, in_specs=in_specs, out_specs=out_specs, check_vma=False)
```

time: 267 us -> 44 us (0.16)
  waiting for transfers between devices: 217 us -> 13 us
  matrix products: 30.8 us -> 0 us
  starting transfers between devices: 0.22 us -> 18.7 us
  between operations: 13.5 us -> 0.28 us
  Pallas kernels: 0 us -> 11.7 us
  local copies, waits for them, and re-layouts: 4.7 us -> 0.01 us
    psum x2 -> x0, waiting for transfers between devices: 217 us -> none  [body(): summed = lax.psum(partial_value, 'row')]
    dot_general x6 -> x0, matrix products: 30.8 us -> none  [hdot(): jnp.dot(left, right, precision=lax.Precision.HIGHEST, preferred_element_t...]
    ppermute x0 -> x10, starting transfers between devices: none -> 18.7 us  [the longest x6 9.31 us: sums_over_row(): parts = [part + lax.ppermute(part, 'row', step) for part in parts]]
    ppermute x0 -> x10, waiting for transfers between devices: none -> 13 us  [the longest x6 11.2 us: sums_over_row(): parts = [part + lax.ppermute(part, 'row', step) for part in parts]]
    pallas_call x0 -> x4, Pallas kernels: none -> 11.7 us  [the longest x1 4.66 us: body(): call(products_kernel, [HBM, HBM], [product, product, halves, halves, whol...]
    sub x1 -> x0, local copies, waits for them, and re-layouts: 2.88 us -> none  [body(): current = current - hdot(vblock, hdot(tfactors[index], summed))]
  transfers between devices with their start and end apart: 2 -> 10, of which waited for: 2 -> 7; matrix products, arithmetic and copies ran while one was open for 1% -> 0% of each run, Pallas kernels for 0% -> 0%
where the time goes in v2:
time: 44 us; the launch traced here: 43.9 us
  starting transfers between devices  18.7 us (42%)
  waiting for transfers between devices  13 us (30%)
  Pallas kernels  11.7 us (27%)
    ppermute x6, waiting for transfers between devices, sums_over_row(): parts = [part + lax.ppermute(part, 'row', step) for part in parts]  11.2 us
    ppermute x6, starting transfers between devices, sums_over_row(): parts = [part + lax.ppermute(part, 'row', step) for part in parts]  9.31 us
    ppermute x2, starting transfers between devices, sums_over_row(): other = lax.ppermute(part, 'row', swap)  5.91 us
    pallas_call x1, Pallas kernels, body(): call(products_kernel, [HBM, HBM], [product, product, halves, halves, whol...  4.66 us
    ppermute x2, starting transfers between devices, sums_over_row(): lax.ppermute(jnp.where(even, two, one), 'row', swap)  3.43 us
    pallas_call x1, Pallas kernels, body(): call(tail_kernel, [VMEM] * 7, [result], scratch, 16, work)  3.16 us
    pallas_call x1, Pallas kernels, body(): call(lead_kernel, [VMEM] * 5, [product, whole], [], 16, work)  2.08 us
    pallas_call x1, Pallas kernels, body(): call(gram_kernel, [VMEM] * 2, [product, product], [], 16, 2 * work)  1.83 us
  transfers between devices with their start and end apart: 10, of which 7 were waited for; matrix products, arithmetic and copies ran while one was open for 0% of the time, Pallas kernels for 0%

profile of v2, /device:TPU:1, one launch (start us, length us, event | category | flops | bytes accessed | tf_op | source)
XLA Modules:
  0.0 43.9 jit_solution(2846376589517672732)
XLA Ops:
  0.0 4.7 %shard_map.37 = (f32[128,256]{1,0:T(8,128)S(1)}, f32[128,256]{1,0:T(8,128)S(1)}, bf16[2,4096,256]{2,1,0:T(8,128)(2,1)S(1)}, bf16[2,4096,256]{2,1,0:T(8,128)(2,1)S(1)}, f32[4096,128]{1,0:T(8,128)S(1)}) custom-call(f32[4096,128]{1,0:T(8,128)} %z_hbm.1, f32[2,4096,256]{2,1,0:T(8,128)} %v_hbm.1), custom_call_target="tpu_custom_call" | custom-call | flops 1610612736 | bytes 4194304 | tf_op jit(solution)/shard_map/pallas_call | solution.py:155
  4.7 1.8 %shard_map.39 = (f32[128,256]{1,0:T(8,128)S(1)}, f32[128,256]{1,0:T(8,128)S(1)}) custom-call(bf16[2,4096,256]{2,1,0:T(8,128)(2,1)S(1)} %get-tuple-element.15.high_ref, bf16[2,4096,256]{2,1,0:T(8,128)(2,1)S(1)} %get-tuple-element.16.low_ref), custom_call_target="tpu_custom_call" | custom-call | flops 1610612736 | bytes 4194304 | tf_op jit(solution)/shard_map/pallas_call | solution.py:163
  6.5 3.3 %collective-permute-start.5 = (f32[128,256]{1,0:T(8,128)S(1)}, f32[128,256]{1,0:T(8,128)S(1)}, u32[]{:S(2)}, u32[]{:S(2)}) collective-permute-start(f32[128,256]{1,0:T(8,128)S(1)} %broadcast_select_fusion.2), channel_id=1, source_target_pairs={{0,16},{16,0},{32,48},{48,32},{64,80},{80,64},{96,112},{112,96},{1... | collective-permute-start | bytes 393224 | tf_op jit(solution)/shard_map/ppermute | solution.py:138
  9.9 0.1 collective-permute-start
  10.0 0.9 %collective-permute-done.5 = f32[128,256]{1,0:T(8,128)S(1)} collective-permute-done((f32[128,256]{1,0:T(8,128)S(1)}, f32[128,256]{1,0:T(8,128)S(1)}, u32[]{:S(2)}, u32[]{:S(2)}) %collective-permute-start.5) | collective-permute-done | bytes 131104 | tf_op jit(solution)/shard_map/ppermute | solution.py:138
  10.9 3.9 %collective-permute-start.6 = (f32[128,256]{1,0:T(8,128)S(1)}, f32[128,256]{1,0:T(8,128)S(1)}, u32[]{:S(2)}, u32[]{:S(2)}) collective-permute-start(f32[128,256]{1,0:T(8,128)S(1)} %select_add_fusion), channel_id=1, source_target_pairs={{0,32},{16,240},{32,0},{48,80},{64,96},{80,48},{96,64},{112,144},{... | collective-permute-start | bytes 393224 | tf_op jit(solution)/shard_map/ppermute | solution.py:140
  14.8 0.0 collective-permute-done
  14.8 0.0 copy-start
  14.8 0.4 collective-permute-start.1
  15.3 1.9 %collective-permute-done.6 = f32[128,256]{1,0:T(8,128)S(1)} collective-permute-done((f32[128,256]{1,0:T(8,128)S(1)}, f32[128,256]{1,0:T(8,128)S(1)}, u32[]{:S(2)}, u32[]{:S(2)}) %collective-permute-start.6) | collective-permute-done | bytes 131104 | tf_op jit(solution)/shard_map/ppermute | solution.py:140
  17.2 0.1 collective-permute-start.7
  17.3 2.7 %collective-permute-done.1 = f32[128,256]{1,0:T(8,128)S(1)} collective-permute-done((f32[128,256]{1,0:T(8,128)S(1)}, f32[128,256]{1,0:T(8,128)S(1)}, u32[]{:S(2)}, u32[]{:S(2)}) %collective-permute-start.1) | collective-permute-done | bytes 131104 | tf_op jit(solution)/shard_map/ppermute | solution.py:140
  20.0 0.1 collective-permute-start.2
  20.1 1.0 %collective-permute-done.7 = f32[128,256]{1,0:T(8,128)S(1)} collective-permute-done((f32[128,256]{1,0:T(8,128)S(1)}, f32[128,256]{1,0:T(8,128)S(1)}, u32[]{:S(2)}, u32[]{:S(2)}) %collective-permute-start.7) | collective-permute-done | bytes 131104 | tf_op jit(solution)/shard_map/ppermute | solution.py:140
  21.1 2.9 %collective-permute-start.8 = (f32[128,256]{1,0:T(8,128)S(1)}, f32[128,256]{1,0:T(8,128)S(1)}, u32[]{:S(2)}, u32[]{:S(2)}) collective-permute-start(f32[128,256]{1,0:T(8,128)S(1)} %add.35), channel_id=1, source_target_pairs={{0,96},{16,176},{32,192},{48,144},{64,160},{80,240},{96,0},{112,20... | collective-permute-start | bytes 393224 | tf_op jit(solution)/shard_map/ppermute | solution.py:140
  24.0 0.0 collective-permute-done.2
  24.1 1.8 %collective-permute-start.3 = (f32[128,256]{1,0:T(8,128)S(1)}, f32[128,256]{1,0:T(8,128)S(1)}, u32[]{:S(2)}, u32[]{:S(2)}) collective-permute-start(f32[128,256]{1,0:T(8,128)S(1)} %add.31), channel_id=1, source_target_pairs={{0,96},{16,176},{32,192},{48,144},{64,160},{80,240},{96,0},{112,20... | collective-permute-start | bytes 393224 | tf_op jit(solution)/shard_map/ppermute | solution.py:140
  25.9 2.3 %collective-permute-done.8 = f32[128,256]{1,0:T(8,128)S(1)} collective-permute-done((f32[128,256]{1,0:T(8,128)S(1)}, f32[128,256]{1,0:T(8,128)S(1)}, u32[]{:S(2)}, u32[]{:S(2)}) %collective-permute-start.8) | collective-permute-done | bytes 131104 | tf_op jit(solution)/shard_map/ppermute | solution.py:140
  28.2 4.3 %collective-permute-start.9 = (f32[128,256]{1,0:T(8,128)S(1)}, f32[128,256]{1,0:T(8,128)S(1)}, u32[]{:S(2)}, u32[]{:S(2)}) collective-permute-start(f32[128,256]{1,0:T(8,128)S(1)} %add.36), channel_id=1, source_target_pairs={{0,16},{16,0},{32,48},{48,32},{64,80},{80,64},{96,112},{112,96},{1... | collective-permute-start | bytes 393224 | tf_op jit(solution)/shard_map/ppermute | solution.py:143
  32.5 3.3 %collective-permute-done.3 = f32[128,256]{1,0:T(8,128)S(1)} collective-permute-done((f32[128,256]{1,0:T(8,128)S(1)}, f32[128,256]{1,0:T(8,128)S(1)}, u32[]{:S(2)}, u32[]{:S(2)}) %collective-permute-start.3) | collective-permute-done | bytes 131104 | tf_op jit(solution)/shard_map/ppermute | solution.py:140
  35.9 1.6 %collective-permute-start.4 = (f32[128,256]{1,0:T(8,128)S(1)}, f32[128,256]{1,0:T(8,128)S(1)}, u32[]{:S(2)}, u32[]{:S(2)}) collective-permute-start(f32[128,256]{1,0:T(8,128)S(1)} %add.32), channel_id=1, source_target_pairs={{0,16},{16,0},{32,48},{48,32},{64,80},{80,64},{96,112},{112,96},{1... | collective-permute-start | bytes 393224 | tf_op jit(solution)/shard_map/ppermute | solution.py:143
  37.5 0.0 collective-permute-done.9
  37.6 0.9 %collective-permute-done.4 = f32[128,256]{1,0:T(8,128)S(1)} collective-permute-done((f32[128,256]{1,0:T(8,128)S(1)}, f32[128,256]{1,0:T(8,128)S(1)}, u32[]{:S(2)}, u32[]{:S(2)}) %collective-permute-start.4) | collective-permute-done | bytes 131104 | tf_op jit(solution)/shard_map/ppermute | solution.py:143
  38.5 0.0 copy-done
  38.5 2.1 %shard_map.38 = (f32[128,256]{1,0:T(8,128)S(1)}, f32[4096,128]{1,0:T(8,128)S(1)}) custom-call(f32[4096,128]{1,0:T(8,128)S(1)} %get-tuple-element.14.z_ref, bf16[2,4096,256]{2,1,0:T(8,128)(2,1)S(1)} %get-tuple-element.15.high_ref, bf16[2,4096,256]{2,1,0:T(8,128)(2,1)S(1)} %get-tuple-element.16.low_ref, f32[2,256,256]{2,1,0:T(8,128)S(1)} %copy-done, ...), custom_call_target="tpu_custom_call" | custom-call | flops 805306368 | bytes 4194304 | tf_op jit(solution)/shard_map/pallas_call | solution.py:165
  40.6 3.2 %shard_map.40 = f32[4096,128]{1,0:T(8,128)} custom-call(f32[4096,128]{1,0:T(8,128)S(1)} %get-tuple-element.19.base_ref, bf16[2,4096,256]{2,1,0:T(8,128)(2,1)S(1)} %get-tuple-element.15.high_ref, bf16[2,4096,256]{2,1,0:T(8,128)(2,1)S(1)} %get-tuple-element.16.low_ref, f32[2,256,256]{2,1,0:T(8,128)S(1)} %copy-done, f32[128,256]{1,0:T(8,128)S(1)} %get-tuple-element.20.lead_ref, ...), custom_call_target="tpu_custom_call" | custom-call | flops 805306368 | bytes 4194304 | tf_op jit(solution)/shard_map/pallas_call | solution.py:169
  (13 shorter events, 0.2 us)
Async XLA Ops:
  6.5 4.3 %collective-permute-start.5 = (f32[128,256]{1,0:T(8,128)S(1)}, f32[128,256]{1,0:T(8,128)S(1)}, u32[]{:S(2)}, u32[]{:S(2)}) collective-permute-start(f32[128,256]{1,0:T(8,128)S(1)} %broadcast_select_fusion.2), channel_id=1, source_target_pairs={{0,16},{16,0},{32,48},{48,32},{64,80},{80,64},{96,112},{112,96},{1... | collective-permute-start | bytes 393224 | tf_op jit(solution)/shard_map/ppermute | solution.py:138
  9.9 4.9 %collective-permute-start = (f32[128,256]{1,0:T(8,128)S(1)}, f32[128,256]{1,0:T(8,128)S(1)}, u32[]{:S(2)}, u32[]{:S(2)}) collective-permute-start(f32[128,256]{1,0:T(8,128)S(1)} %broadcast_select_fusion.5), channel_id=1, source_target_pairs={{0,16},{16,0},{32,48},{48,32},{64,80},{80,64},{96,112},{112,96},{1... | collective-permute-start | bytes 393224 | tf_op jit(solution)/shard_map/ppermute | solution.py:138
  10.9 6.3 %collective-permute-start.6 = (f32[128,256]{1,0:T(8,128)S(1)}, f32[128,256]{1,0:T(8,128)S(1)}, u32[]{:S(2)}, u32[]{:S(2)}) collective-permute-start(f32[128,256]{1,0:T(8,128)S(1)} %select_add_fusion), channel_id=1, source_target_pairs={{0,32},{16,240},{32,0},{48,80},{64,96},{80,48},{96,64},{112,144},{... | collective-permute-start | bytes 393224 | tf_op jit(solution)/shard_map/ppermute | solution.py:140
  14.8 23.7 %copy-start = (f32[2,256,256]{2,1,0:T(8,128)S(1)}, f32[2,256,256]{2,1,0:T(8,128)}, u32[]{:S(2)}) copy-start(f32[2,256,256]{2,1,0:T(8,128)} %t_ref.3) | copy-start | bytes 1572868
  14.8 5.1 %collective-permute-start.1 = (f32[128,256]{1,0:T(8,128)S(1)}, f32[128,256]{1,0:T(8,128)S(1)}, u32[]{:S(2)}, u32[]{:S(2)}) collective-permute-start(f32[128,256]{1,0:T(8,128)S(1)} %select_add_fusion.1), channel_id=1, source_target_pairs={{0,32},{16,240},{32,0},{48,80},{64,96},{80,48},{96,64},{112,144},{... | collective-permute-start | bytes 393224 | tf_op jit(solution)/shard_map/ppermute | solution.py:140
  17.2 3.9 %collective-permute-start.7 = (f32[128,256]{1,0:T(8,128)S(1)}, f32[128,256]{1,0:T(8,128)S(1)}, u32[]{:S(2)}, u32[]{:S(2)}) collective-permute-start(f32[128,256]{1,0:T(8,128)S(1)} %add.34), channel_id=1, source_target_pairs={{0,224},{16,48},{32,64},{48,16},{64,32},{80,112},{96,128},{112,80}... | collective-permute-start | bytes 393224 | tf_op jit(solution)/shard_map/ppermute | solution.py:140
  20.0 4.0 %collective-permute-start.2 = (f32[128,256]{1,0:T(8,128)S(1)}, f32[128,256]{1,0:T(8,128)S(1)}, u32[]{:S(2)}, u32[]{:S(2)}) collective-permute-start(f32[128,256]{1,0:T(8,128)S(1)} %add.30), channel_id=1, source_target_pairs={{0,224},{16,48},{32,64},{48,16},{64,32},{80,112},{96,128},{112,80}... | collective-permute-start | bytes 393224 | tf_op jit(solution)/shard_map/ppermute | solution.py:140
  21.1 7.1 %collective-permute-start.8 = (f32[128,256]{1,0:T(8,128)S(1)}, f32[128,256]{1,0:T(8,128)S(1)}, u32[]{:S(2)}, u32[]{:S(2)}) collective-permute-start(f32[128,256]{1,0:T(8,128)S(1)} %add.35), channel_id=1, source_target_pairs={{0,96},{16,176},{32,192},{48,144},{64,160},{80,240},{96,0},{112,20... | collective-permute-start | bytes 393224 | tf_op jit(solution)/shard_map/ppermute | solution.py:140
  24.1 11.8 %collective-permute-start.3 = (f32[128,256]{1,0:T(8,128)S(1)}, f32[128,256]{1,0:T(8,128)S(1)}, u32[]{:S(2)}, u32[]{:S(2)}) collective-permute-start(f32[128,256]{1,0:T(8,128)S(1)} %add.31), channel_id=1, source_target_pairs={{0,96},{16,176},{32,192},{48,144},{64,160},{80,240},{96,0},{112,20... | collective-permute-start | bytes 393224 | tf_op jit(solution)/shard_map/ppermute | solution.py:140
  28.2 9.3 %collective-permute-start.9 = (f32[128,256]{1,0:T(8,128)S(1)}, f32[128,256]{1,0:T(8,128)S(1)}, u32[]{:S(2)}, u32[]{:S(2)}) collective-permute-start(f32[128,256]{1,0:T(8,128)S(1)} %add.36), channel_id=1, source_target_pairs={{0,16},{16,0},{32,48},{48,32},{64,80},{80,64},{96,112},{112,96},{1... | collective-permute-start | bytes 393224 | tf_op jit(solution)/shard_map/ppermute | solution.py:143
  35.9 2.6 %collective-permute-start.4 = (f32[128,256]{1,0:T(8,128)S(1)}, f32[128,256]{1,0:T(8,128)S(1)}, u32[]{:S(2)}, u32[]{:S(2)}) collective-permute-start(f32[128,256]{1,0:T(8,128)S(1)} %add.32), channel_id=1, source_target_pairs={{0,16},{16,0},{32,48},{48,32},{64,80},{80,64},{96,112},{112,96},{1... | collective-permute-start | bytes 393224 | tf_op jit(solution)/shard_map/ppermute | solution.py:143

commit v3 on v2

--- a/solution.py
+++ b/solution.py
@@ -12,6 +12,7 @@
 HBM = pl.BlockSpec(memory_space=pl.ANY)
 VMEM = pl.BlockSpec(memory_space=pltpu.VMEM)
 CHUNKS = 8
+OUT_CHUNKS = 16
 MIB = 2**20
 
 
@@ -24,9 +25,13 @@
     return jnp.dot(left, right, preferred_element_type=F32)
 
 
-def exact(left, right, right_dim):
+def small(left, right, right_dim):
     dims = (((1,), (right_dim,)), ((), ()))
-    return lax.dot_general(left, right, dims, precision=lax.Precision.HIGHEST, preferred_element_type=F32)
+    left_high, left_low = split(left)
+    right_high, right_low = split(right)
+    rows = left.shape[0]
+    both = lax.dot_general(jnp.concatenate([left_high, left_low], 0), right_high, dims, preferred_element_type=F32)
+    return both[:rows] + both[rows:] + lax.dot_general(left_high, right_low, dims, preferred_element_type=F32)
 
 
 def call(kernel, ins, outs, scratch, limit, flops):
@@ -64,7 +69,7 @@
     second_ref[...] = totals[0]
 
 
-def gram_kernel(high_ref, low_ref, upper_ref, lower_ref):
+def gram_kernel(high_ref, low_ref, after_hbm, upper_ref, lower_ref):
     rows = high_ref.shape[1] // CHUNKS
     total = None
     for k in range(CHUNKS):
@@ -87,7 +92,7 @@
 
 
 def lead_kernel(z_ref, high_ref, low_ref, t_ref, first_ref, lead_ref, base_ref):
-    lead = exact(first_ref[...], t_ref[1], 1)
+    lead = small(first_ref[...], t_ref[1], 1)
     lead_ref[...] = lead
     wide = widened(lead)
     rows = z_ref.shape[0] // CHUNKS
@@ -97,11 +102,11 @@
 
 
 def tail_kernel(base_ref, high_ref, low_ref, t_ref, lead_ref, second_ref, gram_ref, out_hbm, out_ref, sems):
-    tail = exact(second_ref[...] - exact(lead_ref[...], gram_ref[...], 0), t_ref[0], 1)
+    tail = small(second_ref[...] - small(lead_ref[...], gram_ref[...], 0), t_ref[0], 1)
     wide = widened(tail)
-    rows = base_ref.shape[0] // CHUNKS
+    rows = base_ref.shape[0] // OUT_CHUNKS
     copies = []
-    for k in range(CHUNKS):
+    for k in range(OUT_CHUNKS):
         part = pl.ds(k * rows, rows)
         out_ref[part, :] = updated(base_ref[part, :], high_ref[0, part, :], low_ref[0, part, :], wide)
         copy = pltpu.make_async_copy(out_ref.at[part], out_hbm.at[part], sems.at[k])
@@ -131,18 +136,26 @@
     return z - 3 if z % 2 == 0 else z + 3
 
 
-def sums_over_row(pairs, chips):
+CHIPS = 8
+SWAP = [(i, i ^ 1) for i in range(2 * CHIPS)]
+STEPS = [pairs_of(aligned, shifted, CHIPS), pairs_of(shifted, aligned, CHIPS), pairs_of(across, across_back, CHIPS)]
+
+
+def half_sum(one, two):
     even = lax.axis_index("row") % 2 == 0
-    swap = [(i, i ^ 1) for i in range(2 * chips)]
-    steps = [pairs_of(aligned, shifted, chips), pairs_of(shifted, aligned, chips), pairs_of(across, across_back, chips)]
-    parts = [jnp.where(even, one, two) + lax.ppermute(jnp.where(even, two, one), "row", swap) for one, two in pairs]
-    for step in steps:
-        parts = [part + lax.ppermute(part, "row", step) for part in parts]
-    results = []
-    for part in parts:
-        other = lax.ppermute(part, "row", swap)
-        results.append((jnp.where(even, part, other), jnp.where(even, other, part)))
-    return results
+    return jnp.where(even, one, two) + lax.ppermute(jnp.where(even, two, one), "row", SWAP)
+
+
+def sum_along_z(part):
+    for step in STEPS:
+        part = part + lax.ppermute(part, "row", step)
+    return part
+
+
+def both_halves(part):
+    even = lax.axis_index("row") % 2 == 0
+    other = lax.ppermute(part, "row", SWAP)
+    return jnp.where(even, part, other), jnp.where(even, other, part)
 
 
 def body(zblock, reflectors, tfactors):
@@ -160,12 +173,15 @@
         44,
         2 * work,
     )(zblock, reflectors)
-    upper, lower = call(gram_kernel, [VMEM] * 2, [product, product], [], 16, 2 * work)(high, low)
-    (first, second), (upper, lower) = sums_over_row([(first, second), (upper, lower)], 8)
+    part = half_sum(first, second)
+    upper, lower = call(gram_kernel, [VMEM, VMEM, HBM], [product, product], [], 16, 2 * work)(high, low, part)
+    gram_part = half_sum(upper, lower)
+    first, second = both_halves(sum_along_z(part))
+    upper, lower = both_halves(sum_along_z(gram_part))
     lead, base = call(lead_kernel, [VMEM] * 5, [product, whole], [], 16, work)(zblock, high, low, tfactors, first)
     gram = jnp.concatenate([upper, lower], 0)
     result = jax.ShapeDtypeStruct(zblock.shape, F32)
-    scratch = [whole, pltpu.SemaphoreType.DMA((CHUNKS,))]
+    scratch = [whole, pltpu.SemaphoreType.DMA((OUT_CHUNKS,))]
     return call(tail_kernel, [VMEM] * 7, [result], scratch, 16, work)(base, high, low, tfactors, lead, second, gram)[0]
 
 

time: 44 us -> 41.2 us (0.936)
  waiting for transfers between devices: 13 us -> 11.9 us
  Pallas kernels: 11.7 us -> 10.8 us
  starting transfers between devices: 18.7 us -> 17.9 us
    ppermute x10, waiting for transfers between devices: 13 us -> 11.9 us  [the longest x6 10.9 us: sum_along_z(): part = part + lax.ppermute(part, 'row', step)]
    ppermute x10, starting transfers between devices: 18.7 us -> 17.9 us  [the longest x6 9.86 us: sum_along_z(): part = part + lax.ppermute(part, 'row', step)]
    pallas_call x1, Pallas kernels: 3.16 us -> 2.61 us  [body(): call(tail_kernel, [VMEM] * 7, [result], scratch, 16, work)]
  transfers between devices with their start and end apart: 10 -> 10, of which waited for: 7 -> 6; matrix products, arithmetic and copies ran while one was open for 0% -> 0% of each run, Pallas kernels for 0% -> 4%
where the time goes in v3:
time: 41.2 us; the launch traced here: 41.1 us
  starting transfers between devices  17.9 us (43%)
  waiting for transfers between devices  11.9 us (29%)
  Pallas kernels  10.8 us (26%)
    ppermute x6, waiting for transfers between devices, sum_along_z(): part = part + lax.ppermute(part, 'row', step)  10.9 us
    ppermute x6, starting transfers between devices, sum_along_z(): part = part + lax.ppermute(part, 'row', step)  9.86 us
    pallas_call x1, Pallas kernels, body(): call(products_kernel, [HBM, HBM], [product, product, halves, halves, whol...  4.66 us
    ppermute x2, starting transfers between devices, both_halves(): other = lax.ppermute(part, 'row', SWAP)  4.28 us
    ppermute x2, starting transfers between devices, half_sum(): lax.ppermute(jnp.where(even, two, one), 'row', SWAP)  3.78 us
    pallas_call x1, Pallas kernels, body(): call(tail_kernel, [VMEM] * 7, [result], scratch, 16, work)  2.61 us
    pallas_call x1, Pallas kernels, body(): call(gram_kernel, [VMEM, VMEM, HBM], [product, product], [], 16, 2 * work)  1.83 us
    pallas_call x1, Pallas kernels, body(): call(lead_kernel, [VMEM] * 5, [product, whole], [], 16, work)  1.67 us
  transfers between devices with their start and end apart: 10, of which 6 were waited for; matrix products, arithmetic and copies ran while one was open for 0% of the time, Pallas kernels for 4%

profile of v3, /device:TPU:1, one launch (start us, length us, event | category | flops | bytes accessed | tf_op | source)
XLA Modules:
  0.0 41.1 jit_solution(12359513920438864868)
XLA Ops:
  0.0 4.7 %shard_map.37 = (f32[128,256]{1,0:T(8,128)S(1)}, f32[128,256]{1,0:T(8,128)S(1)}, bf16[2,4096,256]{2,1,0:T(8,128)(2,1)S(1)}, bf16[2,4096,256]{2,1,0:T(8,128)(2,1)S(1)}, f32[4096,128]{1,0:T(8,128)S(1)}) custom-call(f32[4096,128]{1,0:T(8,128)} %z_hbm.1, f32[2,4096,256]{2,1,0:T(8,128)} %v_hbm.1), custom_call_target="tpu_custom_call" | custom-call | flops 1610612736 | bytes 4194304 | tf_op jit(solution)/shard_map/pallas_call | solution.py:168
  4.7 3.3 %collective-permute-start = (f32[128,256]{1,0:T(8,128)S(1)}, f32[128,256]{1,0:T(8,128)S(1)}, u32[]{:S(2)}, u32[]{:S(2)}) collective-permute-start(f32[128,256]{1,0:T(8,128)S(1)} %broadcast_select_fusion.5), channel_id=1, source_target_pairs={{0,16},{16,0},{32,48},{48,32},{64,80},{80,64},{96,112},{112,96},{1... | collective-permute-start | bytes 393224 | tf_op jit(solution)/shard_map/ppermute | solution.py:146
  8.0 1.0 %collective-permute-done = f32[128,256]{1,0:T(8,128)S(1)} collective-permute-done((f32[128,256]{1,0:T(8,128)S(1)}, f32[128,256]{1,0:T(8,128)S(1)}, u32[]{:S(2)}, u32[]{:S(2)}) %collective-permute-start) | collective-permute-done | bytes 131104 | tf_op jit(solution)/shard_map/ppermute | solution.py:146
  9.0 1.8 %shard_map.39 = (f32[128,256]{1,0:T(8,128)S(1)}, f32[128,256]{1,0:T(8,128)S(1)}) custom-call(bf16[2,4096,256]{2,1,0:T(8,128)(2,1)S(1)} %get-tuple-element.15.high_ref, bf16[2,4096,256]{2,1,0:T(8,128)(2,1)S(1)} %get-tuple-element.16.low_ref, f32[128,256]{1,0:T(8,128)S(1)} %select_add_fusion.1.after_hbm), custom_call_target="tpu_custom_call" | custom-call | flops 1610612736 | bytes 4194304 | tf_op jit(solution)/shard_map/pallas_call | solution.py:177
  10.9 0.0 copy-start
  10.9 0.4 %collective-permute-start.5 = (f32[128,256]{1,0:T(8,128)S(1)}, f32[128,256]{1,0:T(8,128)S(1)}, u32[]{:S(2)}, u32[]{:S(2)}) collective-permute-start(f32[128,256]{1,0:T(8,128)S(1)} %broadcast_select_fusion.2), channel_id=1, source_target_pairs={{0,16},{16,0},{32,48},{48,32},{64,80},{80,64},{96,112},{112,96},{1... | collective-permute-start | bytes 393224 | tf_op jit(solution)/shard_map/ppermute | solution.py:146
  11.4 3.8 %collective-permute-start.1 = (f32[128,256]{1,0:T(8,128)S(1)}, f32[128,256]{1,0:T(8,128)S(1)}, u32[]{:S(2)}, u32[]{:S(2)}) collective-permute-start(f32[128,256]{1,0:T(8,128)S(1)} %select_add_fusion.1.after_hbm), channel_id=1, source_target_pairs={{0,32},{16,240},{32,0},{48,80},{64,96},{80,48},{96,64},{112,144},{... | collective-permute-start | bytes 393224 | tf_op jit(solution)/shard_map/ppermute | solution.py:151
  15.2 0.0 collective-permute-done.5
  15.2 1.1 %collective-permute-start.6 = (f32[128,256]{1,0:T(8,128)S(1)}, f32[128,256]{1,0:T(8,128)S(1)}, u32[]{:S(2)}, u32[]{:S(2)}) collective-permute-start(f32[128,256]{1,0:T(8,128)S(1)} %select_add_fusion), channel_id=1, source_target_pairs={{0,32},{16,240},{32,0},{48,80},{64,96},{80,48},{96,64},{112,144},{... | collective-permute-start | bytes 393224 | tf_op jit(solution)/shard_map/ppermute | solution.py:151
  16.3 1.3 %collective-permute-done.1 = f32[128,256]{1,0:T(8,128)S(1)} collective-permute-done((f32[128,256]{1,0:T(8,128)S(1)}, f32[128,256]{1,0:T(8,128)S(1)}, u32[]{:S(2)}, u32[]{:S(2)}) %collective-permute-start.1) | collective-permute-done | bytes 131104 | tf_op jit(solution)/shard_map/ppermute | solution.py:151
  17.6 0.1 collective-permute-start.2
  17.7 2.7 %collective-permute-done.6 = f32[128,256]{1,0:T(8,128)S(1)} collective-permute-done((f32[128,256]{1,0:T(8,128)S(1)}, f32[128,256]{1,0:T(8,128)S(1)}, u32[]{:S(2)}, u32[]{:S(2)}) %collective-permute-start.6) | collective-permute-done | bytes 131104 | tf_op jit(solution)/shard_map/ppermute | solution.py:151
  20.4 0.1 collective-permute-start.7
  20.5 1.0 %collective-permute-done.2 = f32[128,256]{1,0:T(8,128)S(1)} collective-permute-done((f32[128,256]{1,0:T(8,128)S(1)}, f32[128,256]{1,0:T(8,128)S(1)}, u32[]{:S(2)}, u32[]{:S(2)}) %collective-permute-start.2) | collective-permute-done | bytes 131104 | tf_op jit(solution)/shard_map/ppermute | solution.py:151
  21.5 3.2 %collective-permute-start.3 = (f32[128,256]{1,0:T(8,128)S(1)}, f32[128,256]{1,0:T(8,128)S(1)}, u32[]{:S(2)}, u32[]{:S(2)}) collective-permute-start(f32[128,256]{1,0:T(8,128)S(1)} %add.34), channel_id=1, source_target_pairs={{0,96},{16,176},{32,192},{48,144},{64,160},{80,240},{96,0},{112,20... | collective-permute-start | bytes 393224 | tf_op jit(solution)/shard_map/ppermute | solution.py:151
  24.7 0.0 collective-permute-done.7
  24.7 1.5 %collective-permute-start.8 = (f32[128,256]{1,0:T(8,128)S(1)}, f32[128,256]{1,0:T(8,128)S(1)}, u32[]{:S(2)}, u32[]{:S(2)}) collective-permute-start(f32[128,256]{1,0:T(8,128)S(1)} %add.38), channel_id=1, source_target_pairs={{0,96},{16,176},{32,192},{48,144},{64,160},{80,240},{96,0},{112,20... | collective-permute-start | bytes 393224 | tf_op jit(solution)/shard_map/ppermute | solution.py:151
  26.3 2.3 %collective-permute-done.3 = f32[128,256]{1,0:T(8,128)S(1)} collective-permute-done((f32[128,256]{1,0:T(8,128)S(1)}, f32[128,256]{1,0:T(8,128)S(1)}, u32[]{:S(2)}, u32[]{:S(2)}) %collective-permute-start.3) | collective-permute-done | bytes 131104 | tf_op jit(solution)/shard_map/ppermute | solution.py:151
  28.6 4.0 %collective-permute-start.4 = (f32[128,256]{1,0:T(8,128)S(1)}, f32[128,256]{1,0:T(8,128)S(1)}, u32[]{:S(2)}, u32[]{:S(2)}) collective-permute-start(f32[128,256]{1,0:T(8,128)S(1)} %add.35), channel_id=1, source_target_pairs={{0,16},{16,0},{32,48},{48,32},{64,80},{80,64},{96,112},{112,96},{1... | collective-permute-start | bytes 393224 | tf_op jit(solution)/shard_map/ppermute | solution.py:157
  32.6 3.6 %collective-permute-done.8 = f32[128,256]{1,0:T(8,128)S(1)} collective-permute-done((f32[128,256]{1,0:T(8,128)S(1)}, f32[128,256]{1,0:T(8,128)S(1)}, u32[]{:S(2)}, u32[]{:S(2)}) %collective-permute-start.8) | collective-permute-done | bytes 131104 | tf_op jit(solution)/shard_map/ppermute | solution.py:151
  36.3 0.3 collective-permute-start.9
  36.5 0.0 collective-permute-done.4
  36.6 0.0 copy-done
  36.6 1.7 %shard_map.38 = (f32[128,256]{1,0:T(8,128)S(1)}, f32[4096,128]{1,0:T(8,128)S(1)}) custom-call(f32[4096,128]{1,0:T(8,128)S(1)} %get-tuple-element.14.z_ref, bf16[2,4096,256]{2,1,0:T(8,128)(2,1)S(1)} %get-tuple-element.15.high_ref, bf16[2,4096,256]{2,1,0:T(8,128)(2,1)S(1)} %get-tuple-element.16.low_ref, f32[2,256,256]{2,1,0:T(8,128)S(1)} %copy-done, ...), custom_call_target="tpu_custom_call" | custom-call | flops 805306368 | bytes 4194304 | tf_op jit(solution)/shard_map/pallas_call | solution.py:181
  38.3 0.0 collective-permute-done.9
  38.3 2.6 %shard_map.40 = f32[4096,128]{1,0:T(8,128)} custom-call(f32[4096,128]{1,0:T(8,128)S(1)} %get-tuple-element.19.base_ref, bf16[2,4096,256]{2,1,0:T(8,128)(2,1)S(1)} %get-tuple-element.15.high_ref, bf16[2,4096,256]{2,1,0:T(8,128)(2,1)S(1)} %get-tuple-element.16.low_ref, f32[2,256,256]{2,1,0:T(8,128)S(1)} %copy-done, f32[128,256]{1,0:T(8,128)S(1)} %get-tuple-element.20.lead_ref, ...), custom_call_target="tpu_custom_call" | custom-call | flops 805306368 | bytes 4194304 | tf_op jit(solution)/shard_map/pallas_call | solution.py:185
  (13 shorter events, 0.3 us)
Async XLA Ops:
  4.7 4.3 %collective-permute-start = (f32[128,256]{1,0:T(8,128)S(1)}, f32[128,256]{1,0:T(8,128)S(1)}, u32[]{:S(2)}, u32[]{:S(2)}) collective-permute-start(f32[128,256]{1,0:T(8,128)S(1)} %broadcast_select_fusion.5), channel_id=1, source_target_pairs={{0,16},{16,0},{32,48},{48,32},{64,80},{80,64},{96,112},{112,96},{1... | collective-permute-start | bytes 393224 | tf_op jit(solution)/shard_map/ppermute | solution.py:146
  10.9 25.7 %copy-start = (f32[2,256,256]{2,1,0:T(8,128)S(1)}, f32[2,256,256]{2,1,0:T(8,128)}, u32[]{:S(2)}) copy-start(f32[2,256,256]{2,1,0:T(8,128)} %t_ref.3) | copy-start | bytes 1572868
  10.9 4.3 %collective-permute-start.5 = (f32[128,256]{1,0:T(8,128)S(1)}, f32[128,256]{1,0:T(8,128)S(1)}, u32[]{:S(2)}, u32[]{:S(2)}) collective-permute-start(f32[128,256]{1,0:T(8,128)S(1)} %broadcast_select_fusion.2), channel_id=1, source_target_pairs={{0,16},{16,0},{32,48},{48,32},{64,80},{80,64},{96,112},{112,96},{1... | collective-permute-start | bytes 393224 | tf_op jit(solution)/shard_map/ppermute | solution.py:146
  11.4 6.2 %collective-permute-start.1 = (f32[128,256]{1,0:T(8,128)S(1)}, f32[128,256]{1,0:T(8,128)S(1)}, u32[]{:S(2)}, u32[]{:S(2)}) collective-permute-start(f32[128,256]{1,0:T(8,128)S(1)} %select_add_fusion.1.after_hbm), channel_id=1, source_target_pairs={{0,32},{16,240},{32,0},{48,80},{64,96},{80,48},{96,64},{112,144},{... | collective-permute-start | bytes 393224 | tf_op jit(solution)/shard_map/ppermute | solution.py:151
  15.2 5.1 %collective-permute-start.6 = (f32[128,256]{1,0:T(8,128)S(1)}, f32[128,256]{1,0:T(8,128)S(1)}, u32[]{:S(2)}, u32[]{:S(2)}) collective-permute-start(f32[128,256]{1,0:T(8,128)S(1)} %select_add_fusion), channel_id=1, source_target_pairs={{0,32},{16,240},{32,0},{48,80},{64,96},{80,48},{96,64},{112,144},{... | collective-permute-start | bytes 393224 | tf_op jit(solution)/shard_map/ppermute | solution.py:151
  17.6 3.9 %collective-permute-start.2 = (f32[128,256]{1,0:T(8,128)S(1)}, f32[128,256]{1,0:T(8,128)S(1)}, u32[]{:S(2)}, u32[]{:S(2)}) collective-permute-start(f32[128,256]{1,0:T(8,128)S(1)} %add.33), channel_id=1, source_target_pairs={{0,224},{16,48},{32,64},{48,16},{64,32},{80,112},{96,128},{112,80}... | collective-permute-start | bytes 393224 | tf_op jit(solution)/shard_map/ppermute | solution.py:151
  20.4 4.4 %collective-permute-start.7 = (f32[128,256]{1,0:T(8,128)S(1)}, f32[128,256]{1,0:T(8,128)S(1)}, u32[]{:S(2)}, u32[]{:S(2)}) collective-permute-start(f32[128,256]{1,0:T(8,128)S(1)} %add.37), channel_id=1, source_target_pairs={{0,224},{16,48},{32,64},{48,16},{64,32},{80,112},{96,128},{112,80}... | collective-permute-start | bytes 393224 | tf_op jit(solution)/shard_map/ppermute | solution.py:151
  21.5 7.1 %collective-permute-start.3 = (f32[128,256]{1,0:T(8,128)S(1)}, f32[128,256]{1,0:T(8,128)S(1)}, u32[]{:S(2)}, u32[]{:S(2)}) collective-permute-start(f32[128,256]{1,0:T(8,128)S(1)} %add.34), channel_id=1, source_target_pairs={{0,96},{16,176},{32,192},{48,144},{64,160},{80,240},{96,0},{112,20... | collective-permute-start | bytes 393224 | tf_op jit(solution)/shard_map/ppermute | solution.py:151
  24.7 11.5 %collective-permute-start.8 = (f32[128,256]{1,0:T(8,128)S(1)}, f32[128,256]{1,0:T(8,128)S(1)}, u32[]{:S(2)}, u32[]{:S(2)}) collective-permute-start(f32[128,256]{1,0:T(8,128)S(1)} %add.38), channel_id=1, source_target_pairs={{0,96},{16,176},{32,192},{48,144},{64,160},{80,240},{96,0},{112,20... | collective-permute-start | bytes 393224 | tf_op jit(solution)/shard_map/ppermute | solution.py:151
  28.6 7.9 %collective-permute-start.4 = (f32[128,256]{1,0:T(8,128)S(1)}, f32[128,256]{1,0:T(8,128)S(1)}, u32[]{:S(2)}, u32[]{:S(2)}) collective-permute-start(f32[128,256]{1,0:T(8,128)S(1)} %add.35), channel_id=1, source_target_pairs={{0,16},{16,0},{32,48},{48,32},{64,80},{80,64},{96,112},{112,96},{1... | collective-permute-start | bytes 393224 | tf_op jit(solution)/shard_map/ppermute | solution.py:157
  36.3 2.0 %collective-permute-start.9 = (f32[128,256]{1,0:T(8,128)S(1)}, f32[128,256]{1,0:T(8,128)S(1)}, u32[]{:S(2)}, u32[]{:S(2)}) collective-permute-start(f32[128,256]{1,0:T(8,128)S(1)} %add.39), channel_id=1, source_target_pairs={{0,16},{16,0},{32,48},{48,32},{64,80},{80,64},{96,112},{112,96},{1... | collective-permute-start | bytes 393224 | tf_op jit(solution)/shard_map/ppermute | solution.py:157

commit v4 on v3

--- a/solution.py
+++ b/solution.py
@@ -69,7 +69,7 @@
     second_ref[...] = totals[0]
 
 
-def gram_kernel(high_ref, low_ref, after_hbm, upper_ref, lower_ref):
+def gram_kernel(high_ref, low_ref, upper_ref, lower_ref):
     rows = high_ref.shape[1] // CHUNKS
     total = None
     for k in range(CHUNKS):
@@ -139,6 +139,7 @@
 CHIPS = 8
 SWAP = [(i, i ^ 1) for i in range(2 * CHIPS)]
 STEPS = [pairs_of(aligned, shifted, CHIPS), pairs_of(shifted, aligned, CHIPS), pairs_of(across, across_back, CHIPS)]
+TURNED = [pairs_of(shifted, aligned, CHIPS), pairs_of(aligned, shifted, CHIPS), pairs_of(across_back, across, CHIPS)]
 
 
 def half_sum(one, two):
@@ -146,8 +147,8 @@
     return jnp.where(even, one, two) + lax.ppermute(jnp.where(even, two, one), "row", SWAP)
 
 
-def sum_along_z(part):
-    for step in STEPS:
+def sum_along_z(part, steps):
+    for step in steps:
         part = part + lax.ppermute(part, "row", step)
     return part
 
@@ -174,10 +175,11 @@
         2 * work,
     )(zblock, reflectors)
     part = half_sum(first, second)
-    upper, lower = call(gram_kernel, [VMEM, VMEM, HBM], [product, product], [], 16, 2 * work)(high, low, part)
+    upper, lower = call(gram_kernel, [VMEM, VMEM], [product, product], [], 16, 2 * work)(high, low)
+    _, upper, lower = lax.optimization_barrier((part, upper, lower))
     gram_part = half_sum(upper, lower)
-    first, second = both_halves(sum_along_z(part))
-    upper, lower = both_halves(sum_along_z(gram_part))
+    first, second = both_halves(sum_along_z(part, STEPS))
+    upper, lower = both_halves(sum_along_z(gram_part, TURNED))
     lead, base = call(lead_kernel, [VMEM] * 5, [product, whole], [], 16, work)(zblock, high, low, tfactors, first)
     gram = jnp.concatenate([upper, lower], 0)
     result = jax.ShapeDtypeStruct(zblock.shape, F32)

time: 41.2 us -> 41.3 us (level)
  starting transfers between devices: 17.9 us -> 22.7 us
  waiting for transfers between devices: 11.9 us -> 7.12 us
    ppermute x6, waiting for transfers between devices: 10.9 us -> 6.45 us  [sum_along_z(): part = part + lax.ppermute(part, 'row', step)]
    ppermute x2, starting transfers between devices: 4.28 us -> 8.53 us  [both_halves(): other = lax.ppermute(part, 'row', SWAP)]
    ppermute x2, waiting for transfers between devices: 0.99 us -> 0.01 us  [half_sum(): lax.ppermute(jnp.where(even, two, one), 'row', SWAP)]
    ppermute x6, starting transfers between devices: 9.86 us -> 10.8 us  [sum_along_z(): part = part + lax.ppermute(part, 'row', step)]
    ppermute x2, waiting for transfers between devices: 0.01 us -> 0.67 us  [both_halves(): other = lax.ppermute(part, 'row', SWAP)]
  transfers between devices with their start and end apart: 10 -> 10, of which waited for: 6 -> 5; matrix products, arithmetic and copies ran while one was open for 0% -> 0% of each run, Pallas kernels for 4% -> 8%
where the time goes in v4:
time: 41.3 us; the launch traced here: 41.2 us
  starting transfers between devices  22.7 us (55%)
  Pallas kernels  10.8 us (26%)
  waiting for transfers between devices  7.12 us (17%)
    ppermute x6, starting transfers between devices, sum_along_z(): part = part + lax.ppermute(part, 'row', step)  10.8 us
    ppermute x2, starting transfers between devices, both_halves(): other = lax.ppermute(part, 'row', SWAP)  8.53 us
    ppermute x6, waiting for transfers between devices, sum_along_z(): part = part + lax.ppermute(part, 'row', step)  6.45 us
    pallas_call x1, Pallas kernels, body(): call(products_kernel, [HBM, HBM], [product, product, halves, halves, whol...  4.66 us
    ppermute x2, starting transfers between devices, half_sum(): lax.ppermute(jnp.where(even, two, one), 'row', SWAP)  3.43 us
    pallas_call x1, Pallas kernels, body(): call(tail_kernel, [VMEM] * 7, [result], scratch, 16, work)  2.61 us
    pallas_call x1, Pallas kernels, body(): call(gram_kernel, [VMEM, VMEM], [product, product], [], 16, 2 * work)  1.83 us
    pallas_call x1, Pallas kernels, body(): call(lead_kernel, [VMEM] * 5, [product, whole], [], 16, work)  1.67 us
  transfers between devices with their start and end apart: 10, of which 5 were waited for; matrix products, arithmetic and copies ran while one was open for 0% of the time, Pallas kernels for 8%

profile of v4, /device:TPU:1, one launch (start us, length us, event | category | flops | bytes accessed | tf_op | source)
XLA Modules:
  0.0 41.2 jit_solution(18212496018649591280)
XLA Ops:
  0.0 4.7 %shard_map.37 = (f32[128,256]{1,0:T(8,128)S(1)}, f32[128,256]{1,0:T(8,128)S(1)}, bf16[2,4096,256]{2,1,0:T(8,128)(2,1)S(1)}, bf16[2,4096,256]{2,1,0:T(8,128)(2,1)S(1)}, f32[4096,128]{1,0:T(8,128)S(1)}) custom-call(f32[4096,128]{1,0:T(8,128)} %z_hbm.1, f32[2,4096,256]{2,1,0:T(8,128)} %v_hbm.1), custom_call_target="tpu_custom_call" | custom-call | flops 1610612736 | bytes 4194304 | tf_op jit(solution)/shard_map/pallas_call | solution.py:169
  4.7 3.3 %collective-permute-start = (f32[128,256]{1,0:T(8,128)S(1)}, f32[128,256]{1,0:T(8,128)S(1)}, u32[]{:S(2)}, u32[]{:S(2)}) collective-permute-start(f32[128,256]{1,0:T(8,128)S(1)} %broadcast_select_fusion.5), channel_id=1, source_target_pairs={{0,16},{16,0},{32,48},{48,32},{64,80},{80,64},{96,112},{112,96},{1... | collective-permute-start | bytes 393224 | tf_op jit(solution)/shard_map/ppermute | solution.py:147
  8.0 1.8 %shard_map.39 = (f32[128,256]{1,0:T(8,128)S(1)}, f32[128,256]{1,0:T(8,128)S(1)}) custom-call(bf16[2,4096,256]{2,1,0:T(8,128)(2,1)S(1)} %get-tuple-element.17.high_ref, bf16[2,4096,256]{2,1,0:T(8,128)(2,1)S(1)} %get-tuple-element.18.low_ref), custom_call_target="tpu_custom_call" | custom-call | flops 1610612736 | bytes 4194304 | tf_op jit(solution)/shard_map/pallas_call | solution.py:178
  9.9 0.0 copy-start
  9.9 0.0 collective-permute-done
  9.9 0.1 collective-permute-start.5
  10.0 3.9 %collective-permute-start.1 = (f32[128,256]{1,0:T(8,128)S(1)}, f32[128,256]{1,0:T(8,128)S(1)}, u32[]{:S(2)}, u32[]{:S(2)}) collective-permute-start(f32[128,256]{1,0:T(8,128)S(1)} %select_add_fusion.1), channel_id=1, source_target_pairs={{0,32},{16,240},{32,0},{48,80},{64,96},{80,48},{96,64},{112,144},{... | collective-permute-start | bytes 393224 | tf_op jit(solution)/shard_map/ppermute | solution.py:152
  14.0 0.0 collective-permute-done.5
  14.0 0.1 collective-permute-start.6
  14.1 2.2 %collective-permute-done.1 = f32[128,256]{1,0:T(8,128)S(1)} collective-permute-done((f32[128,256]{1,0:T(8,128)S(1)}, f32[128,256]{1,0:T(8,128)S(1)}, u32[]{:S(2)}, u32[]{:S(2)}) %collective-permute-start.1) | collective-permute-done | bytes 131104 | tf_op jit(solution)/shard_map/ppermute | solution.py:152
  16.3 0.1 collective-permute-start.2
  16.4 1.8 %collective-permute-done.6 = f32[128,256]{1,0:T(8,128)S(1)} collective-permute-done((f32[128,256]{1,0:T(8,128)S(1)}, f32[128,256]{1,0:T(8,128)S(1)}, u32[]{:S(2)}, u32[]{:S(2)}) %collective-permute-start.6) | collective-permute-done | bytes 131104 | tf_op jit(solution)/shard_map/ppermute | solution.py:152
  18.2 2.2 %collective-permute-start.7 = (f32[128,256]{1,0:T(8,128)S(1)}, f32[128,256]{1,0:T(8,128)S(1)}, u32[]{:S(2)}, u32[]{:S(2)}) collective-permute-start(f32[128,256]{1,0:T(8,128)S(1)} %add.37), channel_id=1, source_target_pairs={{0,32},{16,240},{32,0},{48,80},{64,96},{80,48},{96,64},{112,144},{... | collective-permute-start | bytes 393224 | tf_op jit(solution)/shard_map/ppermute | solution.py:152
  20.5 0.0 collective-permute-done.2
  20.5 2.7 %collective-permute-start.3 = (f32[128,256]{1,0:T(8,128)S(1)}, f32[128,256]{1,0:T(8,128)S(1)}, u32[]{:S(2)}, u32[]{:S(2)}) collective-permute-start(f32[128,256]{1,0:T(8,128)S(1)} %add.34), channel_id=1, source_target_pairs={{0,96},{16,176},{32,192},{48,144},{64,160},{80,240},{96,0},{112,20... | collective-permute-start | bytes 393224 | tf_op jit(solution)/shard_map/ppermute | solution.py:152
  23.2 1.2 %collective-permute-done.7 = f32[128,256]{1,0:T(8,128)S(1)} collective-permute-done((f32[128,256]{1,0:T(8,128)S(1)}, f32[128,256]{1,0:T(8,128)S(1)}, u32[]{:S(2)}, u32[]{:S(2)}) %collective-permute-start.7) | collective-permute-done | bytes 131104 | tf_op jit(solution)/shard_map/ppermute | solution.py:152
  24.4 1.7 %collective-permute-start.8 = (f32[128,256]{1,0:T(8,128)S(1)}, f32[128,256]{1,0:T(8,128)S(1)}, u32[]{:S(2)}, u32[]{:S(2)}) collective-permute-start(f32[128,256]{1,0:T(8,128)S(1)} %add.38), channel_id=1, source_target_pairs={{0,160},{16,112},{32,128},{48,208},{64,224},{80,176},{96,192},{112... | collective-permute-start | bytes 393224 | tf_op jit(solution)/shard_map/ppermute | solution.py:152
  26.1 1.3 %collective-permute-done.3 = f32[128,256]{1,0:T(8,128)S(1)} collective-permute-done((f32[128,256]{1,0:T(8,128)S(1)}, f32[128,256]{1,0:T(8,128)S(1)}, u32[]{:S(2)}, u32[]{:S(2)}) %collective-permute-start.3) | collective-permute-done | bytes 131104 | tf_op jit(solution)/shard_map/ppermute | solution.py:152
  27.4 8.2 %collective-permute-start.4 = (f32[128,256]{1,0:T(8,128)S(1)}, f32[128,256]{1,0:T(8,128)S(1)}, u32[]{:S(2)}, u32[]{:S(2)}) collective-permute-start(f32[128,256]{1,0:T(8,128)S(1)} %add.35), channel_id=1, source_target_pairs={{0,16},{16,0},{32,48},{48,32},{64,80},{80,64},{96,112},{112,96},{1... | collective-permute-start | bytes 393224 | tf_op jit(solution)/shard_map/ppermute | solution.py:158
  35.7 0.0 collective-permute-done.8
  35.7 0.3 collective-permute-start.9
  36.0 0.7 %collective-permute-done.4 = f32[128,256]{1,0:T(8,128)S(1)} collective-permute-done((f32[128,256]{1,0:T(8,128)S(1)}, f32[128,256]{1,0:T(8,128)S(1)}, u32[]{:S(2)}, u32[]{:S(2)}) %collective-permute-start.4) | collective-permute-done | bytes 131104 | tf_op jit(solution)/shard_map/ppermute | solution.py:158
  36.7 0.0 copy-done
  36.7 1.7 %shard_map.38 = (f32[128,256]{1,0:T(8,128)S(1)}, f32[4096,128]{1,0:T(8,128)S(1)}) custom-call(f32[4096,128]{1,0:T(8,128)S(1)} %get-tuple-element.16.z_ref, bf16[2,4096,256]{2,1,0:T(8,128)(2,1)S(1)} %get-tuple-element.17.high_ref, bf16[2,4096,256]{2,1,0:T(8,128)(2,1)S(1)} %get-tuple-element.18.low_ref, f32[2,256,256]{2,1,0:T(8,128)S(1)} %copy-done, ...), custom_call_target="tpu_custom_call" | custom-call | flops 805306368 | bytes 4194304 | tf_op jit(solution)/shard_map/pallas_call | solution.py:183
  38.3 0.0 collective-permute-done.9
  38.4 2.6 %shard_map.40 = f32[4096,128]{1,0:T(8,128)} custom-call(f32[4096,128]{1,0:T(8,128)S(1)} %get-tuple-element.21.base_ref, bf16[2,4096,256]{2,1,0:T(8,128)(2,1)S(1)} %get-tuple-element.17.high_ref, bf16[2,4096,256]{2,1,0:T(8,128)(2,1)S(1)} %get-tuple-element.18.low_ref, f32[2,256,256]{2,1,0:T(8,128)S(1)} %copy-done, f32[128,256]{1,0:T(8,128)S(1)} %get-tuple-element.22.lead_ref, ...), custom_call_target="tpu_custom_call" | custom-call | flops 805306368 | bytes 4194304 | tf_op jit(solution)/shard_map/pallas_call | solution.py:187
  (13 shorter events, 0.3 us)
Async XLA Ops:
  4.7 5.2 %collective-permute-start = (f32[128,256]{1,0:T(8,128)S(1)}, f32[128,256]{1,0:T(8,128)S(1)}, u32[]{:S(2)}, u32[]{:S(2)}) collective-permute-start(f32[128,256]{1,0:T(8,128)S(1)} %broadcast_select_fusion.5), channel_id=1, source_target_pairs={{0,16},{16,0},{32,48},{48,32},{64,80},{80,64},{96,112},{112,96},{1... | collective-permute-start | bytes 393224 | tf_op jit(solution)/shard_map/ppermute | solution.py:147
  9.9 26.8 %copy-start = (f32[2,256,256]{2,1,0:T(8,128)S(1)}, f32[2,256,256]{2,1,0:T(8,128)}, u32[]{:S(2)}) copy-start(f32[2,256,256]{2,1,0:T(8,128)} %t_ref.3) | copy-start | bytes 1572868
  9.9 4.0 %collective-permute-start.5 = (f32[128,256]{1,0:T(8,128)S(1)}, f32[128,256]{1,0:T(8,128)S(1)}, u32[]{:S(2)}, u32[]{:S(2)}) collective-permute-start(f32[128,256]{1,0:T(8,128)S(1)} %broadcast_select_fusion.2), channel_id=1, source_target_pairs={{0,16},{16,0},{32,48},{48,32},{64,80},{80,64},{96,112},{112,96},{1... | collective-permute-start | bytes 393224 | tf_op jit(solution)/shard_map/ppermute | solution.py:147
  10.0 6.3 %collective-permute-start.1 = (f32[128,256]{1,0:T(8,128)S(1)}, f32[128,256]{1,0:T(8,128)S(1)}, u32[]{:S(2)}, u32[]{:S(2)}) collective-permute-start(f32[128,256]{1,0:T(8,128)S(1)} %select_add_fusion.1), channel_id=1, source_target_pairs={{0,32},{16,240},{32,0},{48,80},{64,96},{80,48},{96,64},{112,144},{... | collective-permute-start | bytes 393224 | tf_op jit(solution)/shard_map/ppermute | solution.py:152
  14.0 4.2 %collective-permute-start.6 = (f32[128,256]{1,0:T(8,128)S(1)}, f32[128,256]{1,0:T(8,128)S(1)}, u32[]{:S(2)}, u32[]{:S(2)}) collective-permute-start(f32[128,256]{1,0:T(8,128)S(1)} %select_add_fusion), channel_id=1, source_target_pairs={{0,224},{16,48},{32,64},{48,16},{64,32},{80,112},{96,128},{112,80}... | collective-permute-start | bytes 393224 | tf_op jit(solution)/shard_map/ppermute | solution.py:152
  16.3 4.1 %collective-permute-start.2 = (f32[128,256]{1,0:T(8,128)S(1)}, f32[128,256]{1,0:T(8,128)S(1)}, u32[]{:S(2)}, u32[]{:S(2)}) collective-permute-start(f32[128,256]{1,0:T(8,128)S(1)} %add.33), channel_id=1, source_target_pairs={{0,224},{16,48},{32,64},{48,16},{64,32},{80,112},{96,128},{112,80}... | collective-permute-start | bytes 393224 | tf_op jit(solution)/shard_map/ppermute | solution.py:152
  18.2 6.2 %collective-permute-start.7 = (f32[128,256]{1,0:T(8,128)S(1)}, f32[128,256]{1,0:T(8,128)S(1)}, u32[]{:S(2)}, u32[]{:S(2)}) collective-permute-start(f32[128,256]{1,0:T(8,128)S(1)} %add.37), channel_id=1, source_target_pairs={{0,32},{16,240},{32,0},{48,80},{64,96},{80,48},{96,64},{112,144},{... | collective-permute-start | bytes 393224 | tf_op jit(solution)/shard_map/ppermute | solution.py:152
  20.5 6.9 %collective-permute-start.3 = (f32[128,256]{1,0:T(8,128)S(1)}, f32[128,256]{1,0:T(8,128)S(1)}, u32[]{:S(2)}, u32[]{:S(2)}) collective-permute-start(f32[128,256]{1,0:T(8,128)S(1)} %add.34), channel_id=1, source_target_pairs={{0,96},{16,176},{32,192},{48,144},{64,160},{80,240},{96,0},{112,20... | collective-permute-start | bytes 393224 | tf_op jit(solution)/shard_map/ppermute | solution.py:152
  24.4 11.3 %collective-permute-start.8 = (f32[128,256]{1,0:T(8,128)S(1)}, f32[128,256]{1,0:T(8,128)S(1)}, u32[]{:S(2)}, u32[]{:S(2)}) collective-permute-start(f32[128,256]{1,0:T(8,128)S(1)} %add.38), channel_id=1, source_target_pairs={{0,160},{16,112},{32,128},{48,208},{64,224},{80,176},{96,192},{112... | collective-permute-start | bytes 393224 | tf_op jit(solution)/shard_map/ppermute | solution.py:152
  27.4 9.2 %collective-permute-start.4 = (f32[128,256]{1,0:T(8,128)S(1)}, f32[128,256]{1,0:T(8,128)S(1)}, u32[]{:S(2)}, u32[]{:S(2)}) collective-permute-start(f32[128,256]{1,0:T(8,128)S(1)} %add.35), channel_id=1, source_target_pairs={{0,16},{16,0},{32,48},{48,32},{64,80},{80,64},{96,112},{112,96},{1... | collective-permute-start | bytes 393224 | tf_op jit(solution)/shard_map/ppermute | solution.py:158
  35.7 2.7 %collective-permute-start.9 = (f32[128,256]{1,0:T(8,128)S(1)}, f32[128,256]{1,0:T(8,128)S(1)}, u32[]{:S(2)}, u32[]{:S(2)}) collective-permute-start(f32[128,256]{1,0:T(8,128)S(1)} %add.39), channel_id=1, source_target_pairs={{0,16},{16,0},{32,48},{48,32},{64,80},{80,64},{96,112},{112,96},{1... | collective-permute-start | bytes 393224 | tf_op jit(solution)/shard_map/ppermute | solution.py:158

commit v5 on v4

--- a/solution.py
+++ b/solution.py
@@ -87,8 +87,8 @@
 
 
 def updated(base, high, low, wide):
-    both = mm(high, wide) + mm(low, wide)
-    return base - (both[:, :128] + both[:, 128:])
+    both = mm(high, wide)
+    return base - (both[:, :128] + (both[:, 128:] + mm(low, wide[:, :128])))
 
 
 def lead_kernel(z_ref, high_ref, low_ref, t_ref, first_ref, lead_ref, base_ref):

time: 41.3 us -> 41.2 us (level)
  transfers between devices with their start and end apart: 10 -> 10, of which waited for: 5 -> 5; matrix products, arithmetic and copies ran while one was open for 0% -> 0% of each run, Pallas kernels for 8% -> 9%
where the time goes in v5:
time: 41.2 us; the launch traced here: 41.1 us
  starting transfers between devices  22.7 us (55%)
  Pallas kernels  10.7 us (26%)
  waiting for transfers between devices  7.12 us (17%)
    ppermute x6, starting transfers between devices, sum_along_z(): part = part + lax.ppermute(part, 'row', step)  10.8 us
    ppermute x2, starting transfers between devices, both_halves(): other = lax.ppermute(part, 'row', SWAP)  8.53 us
    ppermute x6, waiting for transfers between devices, sum_along_z(): part = part + lax.ppermute(part, 'row', step)  6.45 us
    pallas_call x1, Pallas kernels, body(): call(products_kernel, [HBM, HBM], [product, product, halves, halves, whol...  4.66 us
    ppermute x2, starting transfers between devices, half_sum(): lax.ppermute(jnp.where(even, two, one), 'row', SWAP)  3.43 us
    pallas_call x1, Pallas kernels, body(): call(tail_kernel, [VMEM] * 7, [result], scratch, 16, work)  2.56 us
    pallas_call x1, Pallas kernels, body(): call(gram_kernel, [VMEM, VMEM], [product, product], [], 16, 2 * work)  1.83 us
    pallas_call x1, Pallas kernels, body(): call(lead_kernel, [VMEM] * 5, [product, whole], [], 16, work)  1.67 us
  transfers between devices with their start and end apart: 10, of which 5 were waited for; matrix products, arithmetic and copies ran while one was open for 0% of the time, Pallas kernels for 9%

profile of v5, /device:TPU:1, one launch (start us, length us, event | category | flops | bytes accessed | tf_op | source)
XLA Modules:
  0.0 41.1 jit_solution(17747123816402122661)
XLA Ops:
  0.0 4.7 %shard_map.37 = (f32[128,256]{1,0:T(8,128)S(1)}, f32[128,256]{1,0:T(8,128)S(1)}, bf16[2,4096,256]{2,1,0:T(8,128)(2,1)S(1)}, bf16[2,4096,256]{2,1,0:T(8,128)(2,1)S(1)}, f32[4096,128]{1,0:T(8,128)S(1)}) custom-call(f32[4096,128]{1,0:T(8,128)} %z_hbm.1, f32[2,4096,256]{2,1,0:T(8,128)} %v_hbm.1), custom_call_target="tpu_custom_call" | custom-call | flops 1610612736 | bytes 4194304 | tf_op jit(solution)/shard_map/pallas_call | solution.py:169
  4.7 3.3 %collective-permute-start = (f32[128,256]{1,0:T(8,128)S(1)}, f32[128,256]{1,0:T(8,128)S(1)}, u32[]{:S(2)}, u32[]{:S(2)}) collective-permute-start(f32[128,256]{1,0:T(8,128)S(1)} %broadcast_select_fusion.5), channel_id=1, source_target_pairs={{0,16},{16,0},{32,48},{48,32},{64,80},{80,64},{96,112},{112,96},{1... | collective-permute-start | bytes 393224 | tf_op jit(solution)/shard_map/ppermute | solution.py:147
  8.0 1.8 %shard_map.39 = (f32[128,256]{1,0:T(8,128)S(1)}, f32[128,256]{1,0:T(8,128)S(1)}) custom-call(bf16[2,4096,256]{2,1,0:T(8,128)(2,1)S(1)} %get-tuple-element.17.high_ref, bf16[2,4096,256]{2,1,0:T(8,128)(2,1)S(1)} %get-tuple-element.18.low_ref), custom_call_target="tpu_custom_call" | custom-call | flops 1610612736 | bytes 4194304 | tf_op jit(solution)/shard_map/pallas_call | solution.py:178
  9.9 0.0 copy-start
  9.9 0.0 collective-permute-done
  9.9 0.1 collective-permute-start.5
  10.0 3.9 %collective-permute-start.1 = (f32[128,256]{1,0:T(8,128)S(1)}, f32[128,256]{1,0:T(8,128)S(1)}, u32[]{:S(2)}, u32[]{:S(2)}) collective-permute-start(f32[128,256]{1,0:T(8,128)S(1)} %select_add_fusion.1), channel_id=1, source_target_pairs={{0,32},{16,240},{32,0},{48,80},{64,96},{80,48},{96,64},{112,144},{... | collective-permute-start | bytes 393224 | tf_op jit(solution)/shard_map/ppermute | solution.py:152
  14.0 0.0 collective-permute-done.5
  14.0 0.1 collective-permute-start.6
  14.1 2.2 %collective-permute-done.1 = f32[128,256]{1,0:T(8,128)S(1)} collective-permute-done((f32[128,256]{1,0:T(8,128)S(1)}, f32[128,256]{1,0:T(8,128)S(1)}, u32[]{:S(2)}, u32[]{:S(2)}) %collective-permute-start.1) | collective-permute-done | bytes 131104 | tf_op jit(solution)/shard_map/ppermute | solution.py:152
  16.3 0.1 collective-permute-start.2
  16.4 1.8 %collective-permute-done.6 = f32[128,256]{1,0:T(8,128)S(1)} collective-permute-done((f32[128,256]{1,0:T(8,128)S(1)}, f32[128,256]{1,0:T(8,128)S(1)}, u32[]{:S(2)}, u32[]{:S(2)}) %collective-permute-start.6) | collective-permute-done | bytes 131104 | tf_op jit(solution)/shard_map/ppermute | solution.py:152
  18.2 2.2 %collective-permute-start.7 = (f32[128,256]{1,0:T(8,128)S(1)}, f32[128,256]{1,0:T(8,128)S(1)}, u32[]{:S(2)}, u32[]{:S(2)}) collective-permute-start(f32[128,256]{1,0:T(8,128)S(1)} %add.37), channel_id=1, source_target_pairs={{0,32},{16,240},{32,0},{48,80},{64,96},{80,48},{96,64},{112,144},{... | collective-permute-start | bytes 393224 | tf_op jit(solution)/shard_map/ppermute | solution.py:152
  20.5 0.0 collective-permute-done.2
  20.5 2.7 %collective-permute-start.3 = (f32[128,256]{1,0:T(8,128)S(1)}, f32[128,256]{1,0:T(8,128)S(1)}, u32[]{:S(2)}, u32[]{:S(2)}) collective-permute-start(f32[128,256]{1,0:T(8,128)S(1)} %add.34), channel_id=1, source_target_pairs={{0,96},{16,176},{32,192},{48,144},{64,160},{80,240},{96,0},{112,20... | collective-permute-start | bytes 393224 | tf_op jit(solution)/shard_map/ppermute | solution.py:152
  23.2 1.2 %collective-permute-done.7 = f32[128,256]{1,0:T(8,128)S(1)} collective-permute-done((f32[128,256]{1,0:T(8,128)S(1)}, f32[128,256]{1,0:T(8,128)S(1)}, u32[]{:S(2)}, u32[]{:S(2)}) %collective-permute-start.7) | collective-permute-done | bytes 131104 | tf_op jit(solution)/shard_map/ppermute | solution.py:152
  24.4 1.7 %collective-permute-start.8 = (f32[128,256]{1,0:T(8,128)S(1)}, f32[128,256]{1,0:T(8,128)S(1)}, u32[]{:S(2)}, u32[]{:S(2)}) collective-permute-start(f32[128,256]{1,0:T(8,128)S(1)} %add.38), channel_id=1, source_target_pairs={{0,160},{16,112},{32,128},{48,208},{64,224},{80,176},{96,192},{112... | collective-permute-start | bytes 393224 | tf_op jit(solution)/shard_map/ppermute | solution.py:152
  26.1 1.3 %collective-permute-done.3 = f32[128,256]{1,0:T(8,128)S(1)} collective-permute-done((f32[128,256]{1,0:T(8,128)S(1)}, f32[128,256]{1,0:T(8,128)S(1)}, u32[]{:S(2)}, u32[]{:S(2)}) %collective-permute-start.3) | collective-permute-done | bytes 131104 | tf_op jit(solution)/shard_map/ppermute | solution.py:152
  27.4 8.2 %collective-permute-start.4 = (f32[128,256]{1,0:T(8,128)S(1)}, f32[128,256]{1,0:T(8,128)S(1)}, u32[]{:S(2)}, u32[]{:S(2)}) collective-permute-start(f32[128,256]{1,0:T(8,128)S(1)} %add.35), channel_id=1, source_target_pairs={{0,16},{16,0},{32,48},{48,32},{64,80},{80,64},{96,112},{112,96},{1... | collective-permute-start | bytes 393224 | tf_op jit(solution)/shard_map/ppermute | solution.py:158
  35.7 0.0 collective-permute-done.8
  35.7 0.3 collective-permute-start.9
  36.0 0.7 %collective-permute-done.4 = f32[128,256]{1,0:T(8,128)S(1)} collective-permute-done((f32[128,256]{1,0:T(8,128)S(1)}, f32[128,256]{1,0:T(8,128)S(1)}, u32[]{:S(2)}, u32[]{:S(2)}) %collective-permute-start.4) | collective-permute-done | bytes 131104 | tf_op jit(solution)/shard_map/ppermute | solution.py:158
  36.7 0.0 copy-done
  36.7 1.7 %shard_map.38 = (f32[128,256]{1,0:T(8,128)S(1)}, f32[4096,128]{1,0:T(8,128)S(1)}) custom-call(f32[4096,128]{1,0:T(8,128)S(1)} %get-tuple-element.16.z_ref, bf16[2,4096,256]{2,1,0:T(8,128)(2,1)S(1)} %get-tuple-element.17.high_ref, bf16[2,4096,256]{2,1,0:T(8,128)(2,1)S(1)} %get-tuple-element.18.low_ref, f32[2,256,256]{2,1,0:T(8,128)S(1)} %copy-done, ...), custom_call_target="tpu_custom_call" | custom-call | flops 805306368 | bytes 4194304 | tf_op jit(solution)/shard_map/pallas_call | solution.py:183
  38.3 0.0 collective-permute-done.9
  38.4 2.6 %shard_map.40 = f32[4096,128]{1,0:T(8,128)} custom-call(f32[4096,128]{1,0:T(8,128)S(1)} %get-tuple-element.21.base_ref, bf16[2,4096,256]{2,1,0:T(8,128)(2,1)S(1)} %get-tuple-element.17.high_ref, bf16[2,4096,256]{2,1,0:T(8,128)(2,1)S(1)} %get-tuple-element.18.low_ref, f32[2,256,256]{2,1,0:T(8,128)S(1)} %copy-done, f32[128,256]{1,0:T(8,128)S(1)} %get-tuple-element.22.lead_ref, ...), custom_call_target="tpu_custom_call" | custom-call | flops 805306368 | bytes 4194304 | tf_op jit(solution)/shard_map/pallas_call | solution.py:187
  (13 shorter events, 0.3 us)
Async XLA Ops:
  4.7 5.2 %collective-permute-start = (f32[128,256]{1,0:T(8,128)S(1)}, f32[128,256]{1,0:T(8,128)S(1)}, u32[]{:S(2)}, u32[]{:S(2)}) collective-permute-start(f32[128,256]{1,0:T(8,128)S(1)} %broadcast_select_fusion.5), channel_id=1, source_target_pairs={{0,16},{16,0},{32,48},{48,32},{64,80},{80,64},{96,112},{112,96},{1... | collective-permute-start | bytes 393224 | tf_op jit(solution)/shard_map/ppermute | solution.py:147
  9.9 26.8 %copy-start = (f32[2,256,256]{2,1,0:T(8,128)S(1)}, f32[2,256,256]{2,1,0:T(8,128)}, u32[]{:S(2)}) copy-start(f32[2,256,256]{2,1,0:T(8,128)} %t_ref.3) | copy-start | bytes 1572868
  9.9 4.0 %collective-permute-start.5 = (f32[128,256]{1,0:T(8,128)S(1)}, f32[128,256]{1,0:T(8,128)S(1)}, u32[]{:S(2)}, u32[]{:S(2)}) collective-permute-start(f32[128,256]{1,0:T(8,128)S(1)} %broadcast_select_fusion.2), channel_id=1, source_target_pairs={{0,16},{16,0},{32,48},{48,32},{64,80},{80,64},{96,112},{112,96},{1... | collective-permute-start | bytes 393224 | tf_op jit(solution)/shard_map/ppermute | solution.py:147
  10.0 6.3 %collective-permute-start.1 = (f32[128,256]{1,0:T(8,128)S(1)}, f32[128,256]{1,0:T(8,128)S(1)}, u32[]{:S(2)}, u32[]{:S(2)}) collective-permute-start(f32[128,256]{1,0:T(8,128)S(1)} %select_add_fusion.1), channel_id=1, source_target_pairs={{0,32},{16,240},{32,0},{48,80},{64,96},{80,48},{96,64},{112,144},{... | collective-permute-start | bytes 393224 | tf_op jit(solution)/shard_map/ppermute | solution.py:152
  14.0 4.2 %collective-permute-start.6 = (f32[128,256]{1,0:T(8,128)S(1)}, f32[128,256]{1,0:T(8,128)S(1)}, u32[]{:S(2)}, u32[]{:S(2)}) collective-permute-start(f32[128,256]{1,0:T(8,128)S(1)} %select_add_fusion), channel_id=1, source_target_pairs={{0,224},{16,48},{32,64},{48,16},{64,32},{80,112},{96,128},{112,80}... | collective-permute-start | bytes 393224 | tf_op jit(solution)/shard_map/ppermute | solution.py:152
  16.3 4.1 %collective-permute-start.2 = (f32[128,256]{1,0:T(8,128)S(1)}, f32[128,256]{1,0:T(8,128)S(1)}, u32[]{:S(2)}, u32[]{:S(2)}) collective-permute-start(f32[128,256]{1,0:T(8,128)S(1)} %add.33), channel_id=1, source_target_pairs={{0,224},{16,48},{32,64},{48,16},{64,32},{80,112},{96,128},{112,80}... | collective-permute-start | bytes 393224 | tf_op jit(solution)/shard_map/ppermute | solution.py:152
  18.2 6.2 %collective-permute-start.7 = (f32[128,256]{1,0:T(8,128)S(1)}, f32[128,256]{1,0:T(8,128)S(1)}, u32[]{:S(2)}, u32[]{:S(2)}) collective-permute-start(f32[128,256]{1,0:T(8,128)S(1)} %add.37), channel_id=1, source_target_pairs={{0,32},{16,240},{32,0},{48,80},{64,96},{80,48},{96,64},{112,144},{... | collective-permute-start | bytes 393224 | tf_op jit(solution)/shard_map/ppermute | solution.py:152
  20.5 6.9 %collective-permute-start.3 = (f32[128,256]{1,0:T(8,128)S(1)}, f32[128,256]{1,0:T(8,128)S(1)}, u32[]{:S(2)}, u32[]{:S(2)}) collective-permute-start(f32[128,256]{1,0:T(8,128)S(1)} %add.34), channel_id=1, source_target_pairs={{0,96},{16,176},{32,192},{48,144},{64,160},{80,240},{96,0},{112,20... | collective-permute-start | bytes 393224 | tf_op jit(solution)/shard_map/ppermute | solution.py:152
  24.4 11.3 %collective-permute-start.8 = (f32[128,256]{1,0:T(8,128)S(1)}, f32[128,256]{1,0:T(8,128)S(1)}, u32[]{:S(2)}, u32[]{:S(2)}) collective-permute-start(f32[128,256]{1,0:T(8,128)S(1)} %add.38), channel_id=1, source_target_pairs={{0,160},{16,112},{32,128},{48,208},{64,224},{80,176},{96,192},{112... | collective-permute-start | bytes 393224 | tf_op jit(solution)/shard_map/ppermute | solution.py:152
  27.4 9.2 %collective-permute-start.4 = (f32[128,256]{1,0:T(8,128)S(1)}, f32[128,256]{1,0:T(8,128)S(1)}, u32[]{:S(2)}, u32[]{:S(2)}) collective-permute-start(f32[128,256]{1,0:T(8,128)S(1)} %add.35), channel_id=1, source_target_pairs={{0,16},{16,0},{32,48},{48,32},{64,80},{80,64},{96,112},{112,96},{1... | collective-permute-start | bytes 393224 | tf_op jit(solution)/shard_map/ppermute | solution.py:158
  35.7 2.7 %collective-permute-start.9 = (f32[128,256]{1,0:T(8,128)S(1)}, f32[128,256]{1,0:T(8,128)S(1)}, u32[]{:S(2)}, u32[]{:S(2)}) collective-permute-start(f32[128,256]{1,0:T(8,128)S(1)} %add.39), channel_id=1, source_target_pairs={{0,16},{16,0},{32,48},{48,32},{64,80},{80,64},{96,112},{112,96},{1... | collective-permute-start | bytes 393224 | tf_op jit(solution)/shard_map/ppermute | solution.py:158
